TPU v7x, 32 devices: a whole 2x2x4 slice. The times are simulated.
32 devices in a mesh: parts: 2 (over y), row: 4 (over z), col: 2 (over x), head: 2 (over core).
Axes of the slice: x: 2, y: 2, z: 4, core: 2. Of those that a mesh axis runs over, the one named last changes fastest.
Arguments:
- pair: bfloat16 [1536, 768, 128], P(('parts', 'row'), 'col'), parts along dimension 0, may hold values from -20 to 20
- crop_length: int32 [2], P('parts'), parts along dimension 0, may hold values from 576 to 768, as said below
- residue_mask: int32 [1536], P('parts'), parts along dimension 0, may hold values from 0 to 1, as said below
- ln_gain: float32 [128], replicated, may hold values from 0.1 to 1.9
- w_query: bfloat16 [128, 128], P(None, 'head'), may hold values from -1 to 1
- w_key: bfloat16 [128, 128], P(None, 'head'), may hold values from -8 to 8
- w_value: bfloat16 [128, 128], P(None, 'head'), may hold values from -0.5 to 0.5
- w_gate: bfloat16 [128, 128], P(None, 'head'), may hold values from -0.5 to 0.5
- gate_bias: float32 [128], P('head'), may hold values from -4 to 4
- w_bias: bfloat16 [128, 4], P(None, 'head'), may hold values from -0.5 to 0.5
- w_out: bfloat16 [128, 128], replicated, may hold values from -1.5 to 1.5
Outputs:
- update: bfloat16 [1536, 768, 128], P(('parts', 'row'), ('col', 'head')), parts along dimension 0
There are 2 independent parts, one for each index of `parts`. A program takes and returns all parts, laid end to end along the dimension named above; an argument that names none is the same for every part. Nothing has to cross between parts.
Inputs may be any that keep to these rules, and one draw needn't show every extreme that they name: `crop_length`: in every odd group the crop fills the whole grid; in every even group it is shorter. `residue_mask`: the first residue is 1.
All inputs are finite; a program needn't handle non-finite values.
Results may differ from a plain program's by a relative error of at most 0.012.
The roundings to bfloat16 on the way count: a program that leaves them out, or rounds other values in their place, can miss the bound.
Values may be sent and summed in bfloat16 or wider, within the bound.
A program may use at most 256 MiB of HBM per device.

v0:
```python
import math

import jax
import jax.numpy as jnp
from jax import lax
from jax.sharding import PartitionSpec as P


def project(block, w_query, w_key, w_value, w_gate, gate_bias, local_heads):
    count, span, width = block.shape
    head_size = w_query.shape[1] // local_heads
    flat = block.reshape(-1, width)
    scale = 1.0 / math.sqrt(head_size)
    query = (jnp.dot(flat, w_query, preferred_element_type=jnp.float32) * scale).astype(
        jnp.bfloat16
    )
    keys = jnp.dot(flat, w_key, preferred_element_type=jnp.float32).astype(jnp.bfloat16)
    values = jnp.dot(flat, w_value, preferred_element_type=jnp.float32).astype(jnp.bfloat16)
    gate = jax.nn.sigmoid(jnp.dot(flat, w_gate, preferred_element_type=jnp.float32) + gate_bias)
    query = query.reshape(count, span, local_heads, head_size)
    gate = gate.reshape(count, span, local_heads, head_size)
    keys = keys.reshape(count, span, w_key.shape[1])
    values = values.reshape(count, span, w_value.shape[1])
    return (query, keys, values, gate)


def attend_rows(
    query, keys_all, values_all, gate, bias_plane, row_ids, key_live, total_len, tile_rows
):
    count, span, local_heads, head_size = query.shape
    local_chan = local_heads * head_size

    def attend_tile(index, gated_all):
        start = index * tile_rows
        q_tile = lax.dynamic_slice_in_dim(query, start, tile_rows, 0)
        k_tile = lax.dynamic_slice_in_dim(keys_all, start, tile_rows, 0)
        v_tile = lax.dynamic_slice_in_dim(values_all, start, tile_rows, 0)
        g_tile = lax.dynamic_slice_in_dim(gate, start, tile_rows, 0)
        ids_tile = lax.dynamic_slice_in_dim(row_ids, start, tile_rows, 0)
        scores = jnp.einsum("bjhd,bkhd->bhjk", q_tile, k_tile, preferred_element_type=jnp.float32)
        scores = scores + bias_plane[None]
        scores = jnp.where(key_live[None, None, None, :], scores, -1000000000.0)
        top = jnp.max(scores, axis=-1, keepdims=True)
        expo = jnp.exp(scores - top)
        total_w = jnp.sum(expo, axis=-1)
        weights = expo.astype(jnp.bfloat16)
        attended = jnp.einsum(
            "bhjk,bkhd->bjhd", weights, v_tile, preferred_element_type=jnp.float32
        )
        attended = attended / jnp.transpose(total_w, (0, 2, 1))[..., None]
        gated = g_tile * attended
        gated = jnp.where((ids_tile < total_len)[:, None, None, None], gated, 0.0)
        gated = gated.astype(jnp.bfloat16).reshape(tile_rows, span, local_chan)
        return lax.dynamic_update_slice_in_dim(gated_all, gated, start, 0)

    live_rows = jnp.sum((row_ids < total_len).astype(jnp.int32))
    tile_count = (live_rows + tile_rows - 1) // tile_rows
    gated_all = jnp.zeros((count, span, local_chan), jnp.bfloat16)
    return lax.fori_loop(0, tile_count, attend_tile, gated_all)


def per_device(
    pair,
    crop_length,
    residue_mask,
    ln_gain,
    w_query,
    w_key,
    w_value,
    w_gate,
    gate_bias,
    w_bias,
    w_out,
):
    rows_here, cols_here, width = pair.shape
    grid_len = residue_mask.shape[0]
    local_heads = w_bias.shape[1]
    head_size = w_query.shape[1] // local_heads
    local_chan = w_query.shape[1]
    row_pos = lax.axis_index("row")
    col_pos = lax.axis_index("col")
    head_pos = lax.axis_index("head")
    as_float = pair.astype(jnp.float32)
    centre = as_float - jnp.mean(as_float, axis=-1, keepdims=True)
    spread = jnp.mean(centre * centre, axis=-1, keepdims=True)
    normed = (centre * lax.rsqrt(spread + 1e-05) * ln_gain).astype(jnp.bfloat16)
    bias_local = jnp.dot(normed.reshape(-1, width), w_bias, preferred_element_type=jnp.float32)
    bias_local = jnp.transpose(
        bias_local.astype(jnp.bfloat16).reshape(rows_here, cols_here, local_heads), (2, 0, 1)
    )
    bias_wide = lax.all_gather(bias_local, "col", axis=2, tiled=True)
    total_len = crop_length[0]
    local_ids = jnp.arange(rows_here, dtype=jnp.int32)
    row_ids = row_pos * rows_here + local_ids
    key_ids = jnp.arange(grid_len, dtype=jnp.int32)
    key_live = (residue_mask == 1) & (key_ids < total_len)
    query, keys_here, values_here, gate = project(
        normed, w_query, w_key, w_value, w_gate, gate_bias, local_heads
    )
    keys_all, values_all = (
        lax.all_gather(keys_here, "col", axis=1, tiled=True),
        lax.all_gather(values_here, "col", axis=1, tiled=True),
    )
    bias_full = lax.all_gather(bias_wide, "row", axis=1, tiled=True)
    bias_plane = lax.dynamic_slice_in_dim(bias_full, col_pos * cols_here, cols_here, 1).astype(
        jnp.float32
    )
    keys_all = keys_all.reshape(rows_here, grid_len, local_heads, head_size)
    values_all = values_all.reshape(rows_here, grid_len, local_heads, head_size)
    gated_all = attend_rows(
        query, keys_all, values_all, gate, bias_plane, row_ids, key_live, total_len, 8
    )
    w_part = lax.dynamic_slice_in_dim(w_out, head_pos * local_chan, local_chan, 0)
    partial_terms = jnp.dot(
        gated_all.reshape(-1, local_chan), w_part, preferred_element_type=jnp.float32
    )
    partial_terms = partial_terms.reshape(rows_here, cols_here, width)
    mixed = lax.psum_scatter(partial_terms, "head", scatter_dimension=1, tiled=True).astype(
        jnp.bfloat16
    )
    return mixed


def solution(mesh):
    placed = (
        P(("parts", "row"), "col", None),
        P("parts"),
        P("parts"),
        P(),
        P(None, "head"),
        P(None, "head"),
        P(None, "head"),
        P(None, "head"),
        P("head"),
        P(None, "head"),
        P(),
    )
    return jax.shard_map(
        per_device,
        mesh=mesh,
        in_specs=placed,
        out_specs=P(("parts", "row"), ("col", "head"), None),
        check_vma=False,
    )
```

profile of v0, /device:TPU:0, one launch (start us, length us, event | category | flops | bytes accessed | tf_op | source)
XLA Modules:
  0.0 1140.8 jit_solution(14499666844636464061)
XLA Ops:
  6.5 12.7 %convert_reduce_fusion = f32[192,384]{1,0:T(8,128)S(1)} fusion(bf16[192,384,128]{2,1,0:T(8,128)(2,1)} %param.13), kind=kLoop, calls=%fused_computation.34 | loop fusion | flops 18800640 | bytes 19169280 | tf_op jit(solution)/shard_map/reduce_sum | solution.py:84
  19.3 22.0 %fusion.35 = f32[192,384]{1,0:T(8,128)S(1)} fusion(bf16[192,384,128]{2,1,0:T(8,128)(2,1)S(1)} %copy-done.2, f32[192,384]{1,0:T(8,128)S(1)} %broadcast_multiply_fusion), kind=kLoop, calls=%fused_computation.37 | loop fusion | flops 37675008 | bytes 19464192 | tf_op jit(solution)/shard_map/reduce_sum | solution.py:85
  41.4 24.0 %fusion.37 = bf16[192,384,128]{2,1,0:T(8,128)(2,1)S(1)} fusion(bf16[192,384,128]{2,1,0:T(8,128)(2,1)} %param.13, f32[128]{0:T(128)S(1)} %copy-done.7, f32[192,384]{1,0:T(8,128)S(1)} %add_rsqrt_fusion, f32[192,384]{1,0:T(8,128)S(1)} %broadcast_multiply_fusion), kind=kLoop, calls=%fused_computation.39 | loop fusion | flops 47185920 | bytes 38339072 | tf_op jit(solution)/shard_map/convert_element_type | solution.py:86
  65.4 6.4 copy-done.1
  76.8 10.7 all_gather.14
  87.6 12.6 %convolution_convert_fusion = bf16[73728,64]{0,1:T(8,128)(2,1)} fusion(bf16[73728,128]{1,0:T(8,128)(2,1)} %bitcast.66, bf16[128,64]{0,1:T(8,128)(2,1)S(1)} %copy-done.3), kind=kOutput, calls=%fused_computation.30 | convolution fusion | flops 1212678144 | bytes 28327936 | tf_op jit(solution)/shard_map/dot_general | solution.py:17
  100.3 9.4 copy.21
  109.9 12.7 %convolution_convert_fusion.1 = bf16[73728,64]{0,1:T(8,128)(2,1)} fusion(bf16[73728,128]{1,0:T(8,128)(2,1)} %bitcast.67, bf16[128,64]{0,1:T(8,128)(2,1)S(1)} %copy-done.4), kind=kOutput, calls=%fused_computation.31 | convolution fusion | flops 1212678144 | bytes 28327936 | tf_op jit(solution)/shard_map/dot_general | solution.py:18
  122.6 9.4 copy.19
  134.1 13.0 %fusion.32 = bf16[73728,64]{0,1:T(8,128)(2,1)} fusion(bf16[73728,128]{1,0:T(8,128)(2,1)} %bitcast.68, bf16[128,64]{0,1:T(8,128)(2,1)S(1)} %copy-done.5), kind=kOutput, calls=%fused_computation.29 | convolution fusion | flops 1217396736 | bytes 28327936 | tf_op jit(solution)/shard_map/dot_general | solution.py:14
  147.1 12.9 %copy.20 = bf16[8,8,192,384]{3,2,1,0:T(8,128)(2,1)} copy(bf16[8,8,192,384]{3,1,2,0:T(8,128)(2,1)} %bitcast.72) | data formatting | bytes 18874368
  160.0 15.2 %fusion.31 = f32[73728,64]{0,1:T(8,128)} fusion(bf16[73728,128]{1,0:T(8,128)(2,1)} %bitcast.69, bf16[128,64]{0,1:T(8,128)(2,1)S(1)} %copy-done.9, f32[64]{0:T(128)S(1)} %copy-done.10), kind=kOutput, calls=%fused_computation.28 | convolution fusion | flops 1226833920 | bytes 37765376 | tf_op jit(solution)/shard_map/dot_general | solution.py:19
  175.2 15.7 %copy.18 = f32[8,8,192,384]{3,2,1,0:T(8,128)} copy(f32[8,8,192,384]{3,1,2,0:T(8,128)} %bitcast.78) | data formatting | bytes 37748736
  192.4 172.1 %all-gather.6.cloned.1.call-done = bf16[192,768,64]{1,0,2:T(8,128)(2,1)} async-done(((bf16[192,384,64]{1,0,2:T(8,128)(2,1)}), bf16[192,768,64]{1,0,2:T(8,128)(2,1)}) %all-gather.6.cloned.1.call-update) | async-done | bytes 18874384 | tf_op jit(solution)/shard_map/all_gather | solution.py:101
  364.5 21.6 %copy.13 = bf16[192,768,64]{1,2,0:T(8,128)(2,1)} copy(bf16[192,768,64]{1,0,2:T(8,128)(2,1)} %all-gather.6.cloned.1.call-done) | data formatting | bytes 37748736 | tf_op jit(solution)/shard_map/all_gather | solution.py:101
  386.1 204.3 %all-gather.4.cloned.1.call-done = bf16[192,768,64]{1,0,2:T(8,128)(2,1)} async-done(((bf16[192,384,64]{1,0,2:T(8,128)(2,1)}), bf16[192,768,64]{1,0,2:T(8,128)(2,1)}) %all-gather.4.cloned.1.call-update) | async-done | bytes 18874384 | tf_op jit(solution)/shard_map/all_gather | solution.py:102
  590.4 20.1 %copy.12 = bf16[192,768,64]{1,2,0:T(8,128)(2,1)} copy(bf16[192,768,64]{1,0,2:T(8,128)(2,1)} %all-gather.4.cloned.1.call-done) | data formatting | bytes 37748736 | tf_op jit(solution)/shard_map/all_gather | solution.py:102
  615.9 440.5 %while.10 = (s32[]{:T(128)}, bf16[192,384,64]{1,2,0:T(8,128)(2,1)}, s32[]{:T(128)}, s32[192]{0:T(256)S(1)}, s32[]{:T(128)}, /*index=5*/f32[192,384,2,32]{1,0,3,2...) while((s32[]{:T(128)}, bf16[192,384,64]{1,2,0:T(8,128)(2,1)}, ...), condition=%wide.region_6.7_spmd, body=%wide.region_3.6_spmd.sunk | while | flops 656658432 | bytes 70117888 | solution.py:59
  866.2 5.9 fusion.64
  921.2 5.9 fusion.64
  976.3 5.9 fusion.64
  1056.3 17.1 %fusion.38 = f32[192,384,128]{2,1,0:T(8,128)} fusion(bf16[192,384,64]{1,2,0:T(8,128)(2,1)} %get-tuple-element.63, bf16[128,128]{1,0:T(8,128)(2,1)S(1)} %copy-done, s32[]{:T(128)S(6)} %select_n.29), kind=kOutput, calls=%fused_computation.44 | convolution fusion | flops 1207959552 | bytes 47202308 | tf_op jit(solution)/shard_map/dot_general | solution.py:114
  1073.5 49.4 %reduce-scatter.2.cloned.1.call-done = f32[192,192,128]{2,1,0:T(8,128)} async-done(((f32[192,384,128]{2,1,0:T(8,128)}), f32[192,192,128]{2,1,0:T(8,128)}) %reduce-scatter.2.cloned.1.call-update) | async-done | bytes 18874384 | tf_op jit(solution)/shard_map/reduce_scatter | solution.py:118
  1122.8 11.4 %convert_element_type.41 = bf16[192,192,128]{2,1,0:T(8,128)(2,1)} convert(f32[192,192,128]{2,1,0:T(8,128)} %reduce-scatter.2.cloned.1.call-done) | non-fusion elementwise | flops 4718592 | bytes 28311552 | tf_op jit(solution)/shard_map/convert_element_type | solution.py:118
  (204 shorter events, 435.1 us)
Async XLA Ops:
  6.5 1049.8 %copy-start = (bf16[128,128]{1,0:T(8,128)(2,1)S(1)}, bf16[128,128]{1,0:T(8,128)(2,1)}, u32[]{:S(2)}) copy-start(bf16[128,128]{1,0:T(8,128)(2,1)} %param.23) | copy-start | bytes 98308
  6.5 34.8 %copy-start.7 = (f32[128]{0:T(128)S(1)}, f32[128]{0:T(128)}, u32[]{:S(2)}) copy-start(f32[128]{0:T(128)} %param.16) | copy-start | bytes 1540
  6.5 184.4 %all-gather.8.cloned.1.call-start = ((), (), s32[]{:S(2)}) async-start(), calls=%async_computation.3 | async-start | bytes 2949120 | tf_op jit(solution)/shard_map/all_gather | solution.py:104
  6.5 12.7 %copy-start.2 = (bf16[192,384,128]{2,1,0:T(8,128)(2,1)S(1)}, bf16[192,384,128]{2,1,0:T(8,128)(2,1)}, u32[]{:S(2)}) copy-start(bf16[192,384,128]{2,1,0:T(8,128)(2,1)} %param.13) | copy-start | bytes 56623108
  41.3 30.5 %copy-start.8 = (bf16[128,2]{0,1:T(2,128)(2,1)S(1)}, bf16[128,2]{0,1:T(2,128)(2,1)}, u32[]{:S(2)}) copy-start(bf16[128,2]{0,1:T(2,128)(2,1)} %param.22) | copy-start | bytes 1540
  65.3 6.5 copy-start.1
  65.3 22.3 %copy-start.3 = (bf16[128,64]{0,1:T(8,128)(2,1)S(1)}, bf16[128,64]{0,1:T(8,128)(2,1)}, u32[]{:S(2)}) copy-start(bf16[128,64]{0,1:T(8,128)(2,1)} %param.18) | copy-start | bytes 49156
  87.6 276.9 %all-gather.6.cloned.1.call-start = ((), (), s32[]{:S(2)}) async-start(), calls=%async_computation.2 | async-start | bytes 28311552 | tf_op jit(solution)/shard_map/all_gather | solution.py:101
  100.3 9.6 copy-start.4
  109.7 480.8 %all-gather.4.cloned.1.call-start = ((), (), s32[]{:S(2)}) async-start(), calls=%async_computation.1 | async-start | bytes 28311552 | tf_op jit(solution)/shard_map/all_gather | solution.py:102
  122.6 11.5 %copy-start.5 = (bf16[128,64]{0,1:T(8,128)(2,1)S(1)}, bf16[128,64]{0,1:T(8,128)(2,1)}, u32[]{:S(2)}) copy-start(bf16[128,64]{0,1:T(8,128)(2,1)} %param.17) | copy-start | bytes 49156
  132.0 990.8 %reduce-scatter.2.cloned.1.call-start = ((), (), s32[]{:S(2)}) async-start(), calls=%async_computation.4 | async-start | bytes 56623104 | tf_op jit(solution)/shard_map/reduce_scatter | solution.py:118
  134.1 25.9 %copy-start.9 = (bf16[128,64]{0,1:T(8,128)(2,1)S(1)}, bf16[128,64]{0,1:T(8,128)(2,1)}, u32[]{:S(2)}) copy-start(bf16[128,64]{0,1:T(8,128)(2,1)} %param.20) | copy-start | bytes 49156
  134.1 25.9 %copy-start.10 = (f32[64]{0:T(128)S(1)}, f32[64]{0:T(128)}, u32[]{:S(2)}) copy-start(f32[64]{0:T(128)} %param.21) | copy-start | bytes 772
  175.2 15.7 %copy-start.6 = (s32[768]{0:T(1024)S(1)}, s32[768]{0:T(1024)}, u32[]{:S(2)}) copy-start(s32[768]{0:T(1024)} %param.15) | copy-start | bytes 9220
Sparse Core Ops, SparseCore 0:
  87.7 51.9 all-gather.7
  141.2 223.1 all-gather.5
  366.0 224.3 all-gather.3
  1073.6 49.1 reduce-scatter.1
where the time goes:
time: 1140 us
  waiting for transfers between devices  426 us (37%)
  matrix products  315 us (28%)
  other arithmetic  200 us (18%)
  local copies, waits for them, and re-layouts  174 us (15%)
  between operations  14.6 us (1%)
    all_gather x1, waiting for transfers between devices, per_device(): lax.all_gather(values_here, 'col', axis=1, tiled=True)  204 us
    all_gather x1, waiting for transfers between devices, per_device(): lax.all_gather(keys_here, 'col', axis=1, tiled=True)  172 us
    dot_general x24, matrix products, attend_tile(): jnp.einsum('bhjk,bkhd->bjhd', weights, v_tile, preferred_element_type=jnp...  140 us
    reduce_sum x24, other arithmetic, attend_tile(): total_w = jnp.sum(expo, axis=-1)  110 us
    dot_general x24, matrix products, attend_tile(): jnp.einsum('bjhd,bkhd->bhjk', q_tile, k_tile, preferred_element_type=jnp....  99 us
    unnamed x27, local copies, waits for them, and re-layouts  54 us
    reduce_scatter x1, waiting for transfers between devices, per_device(): lax.psum_scatter(partial_terms, 'head', scatter_dimension=1, tiled=True)  49.4 us
    dynamic_slice x24, local copies, waits for them, and re-layouts, attend_tile(): g_tile = lax.dynamic_slice_in_dim(gate, start, tile_rows, 0)  28.6 us
  transfers between devices with their start and end apart: 4, of which 3 were waited for; matrix products, arithmetic and copies ran while one was open for 11% of the time, Pallas kernels for 0%

commit v1 on v0

v1 whole, which is shorter than its diff:
```python
import functools
import math

import jax
import jax.numpy as jnp
from jax import lax
from jax.experimental import pallas as pl
from jax.experimental.pallas import tpu as pltpu
from jax.sharding import PartitionSpec as P

NT = (((1,), (1,)), ((), ()))


def layer_norm(block, gain):
    values = block.astype(jnp.float32)
    centre = values - jnp.mean(values, axis=-1, keepdims=True)
    spread = jnp.mean(centre * centre, axis=-1, keepdims=True)
    return (centre * lax.rsqrt(spread + 1e-05) * gain).astype(jnp.bfloat16)


def bias_kernel(pair_ref, gain_ref, w_ref, out_ref):
    heads = out_ref.shape[0]
    for row in range(pair_ref.shape[0]):
        normed = layer_norm(pair_ref[row], gain_ref[...])
        plane = lax.dot_general(w_ref[...], normed, NT, preferred_element_type=jnp.float32)
        out_ref[:, row, :] = plane[:heads]


def pair_bias(pair, gain, w_bias):
    rows, cols, width = pair.shape
    heads = w_bias.shape[1]
    padded = jnp.zeros((8 * pl.cdiv(heads, 8), width), jnp.bfloat16)
    padded = lax.dynamic_update_slice(padded, w_bias.T, (0, 0))
    step = 8
    return pl.pallas_call(
        bias_kernel,
        grid=(rows // step,),
        in_specs=[
            pl.BlockSpec((step, cols, width), lambda i: (i, 0, 0)),
            pl.BlockSpec((1, width), lambda i: (0, 0)),
            pl.BlockSpec(padded.shape, lambda i: (0, 0)),
        ],
        out_specs=pl.BlockSpec((heads, step, cols), lambda i: (0, i, 0)),
        out_shape=jax.ShapeDtypeStruct((heads, rows, cols), jnp.float32),
        cost_estimate=pl.CostEstimate(
            flops=2 * rows * cols * width * 8, bytes_accessed=rows * cols * width * 2, transcendentals=0
        ),
    )(pair, gain, padded)


def attend_kernel(blocks, heads, tile, info_ref, *refs):
    pair_refs = refs[:blocks]
    gain_ref, w_in_ref, gate_bias_ref, w_out_ref, bias_ref, live_ref = refs[blocks : blocks + 6]
    rest = refs[blocks + 6 :]
    out_refs, (bias_all, query_all, keys_all, values_all, gate_all, update_all) = rest[:-6], rest[-6:]
    span, width = keys_all.shape
    cols = pair_refs[0].shape[1]
    head_size = width // heads
    col_pos, place, total_len = info_ref[0], info_ref[1], info_ref[3]
    row_id = info_ref[2] + pl.program_id(0)
    scale = 1.0 / math.sqrt(head_size)

    @pl.when(pl.program_id(0) == 0)
    def _():
        live = live_ref[...] > 0
        for head in range(heads):

            @pl.loop(0, span // 64)
            def _(part):
                rows = pl.ds(pl.multiple_of(part * 64, 64), 64)
                bias_all[head, rows, :] = jnp.where(
                    live, bias_ref[head, rows, :].astype(jnp.float32), -1000000000.0
                )

        values_all[:, width:] = jnp.ones((span, width), jnp.bfloat16)

    for step in range(blocks):
        normed = layer_norm(pair_refs[step][0], gain_ref[...])
        start = jnp.bitwise_xor(col_pos, step) * cols
        rows = pl.ds(pl.multiple_of(start, 32), cols)
        mixed = jnp.dot(normed, w_in_ref[...], preferred_element_type=jnp.float32)
        query_all[rows, :] = (mixed[:, :width] * scale).astype(jnp.bfloat16)
        keys_all[rows, :] = mixed[:, width : 2 * width].astype(jnp.bfloat16)
        values_all[rows, :width] = mixed[:, 2 * width : 3 * width].astype(jnp.bfloat16)
        gate_all[rows, :] = jax.nn.sigmoid(mixed[:, 3 * width :] + gate_bias_ref[...])

    lanes = lax.broadcasted_iota(jnp.int32, (1, width), 1) // head_size
    row_scale = (row_id < total_len).astype(jnp.float32)

    @pl.loop(0, span // tile)
    def _(index):
        rows = pl.ds(pl.multiple_of(index * tile, tile), tile)
        query = query_all[rows, :]
        attended = jnp.zeros((tile, width), jnp.float32)
        for head in range(heads):
            masked = jnp.where(lanes == head, query, jnp.zeros_like(query))
            scores = lax.dot_general(masked, keys_all[...], NT, preferred_element_type=jnp.float32)
            scores = scores + bias_all[head, rows, :]
            top = jnp.max(scores, axis=-1, keepdims=True)
            weights = jnp.exp(scores - top).astype(jnp.bfloat16)
            summed = jnp.dot(weights, values_all[...], preferred_element_type=jnp.float32)
            attended = jnp.where(lanes == head, summed[:, :width] / summed[:, width:], attended)
        gated = gate_all[rows, :] * attended
        gated = jnp.where(row_scale > 0.0, gated, 0.0).astype(jnp.bfloat16)
        update = jnp.dot(gated, w_out_ref[...], preferred_element_type=jnp.float32)
        update_all[rows, :] = update.astype(jnp.bfloat16)

    half = out_refs[0].shape[1]
    for step in range(len(out_refs)):
        start = jnp.bitwise_xor(place, step) * half
        out_refs[step][0] = update_all[pl.ds(pl.multiple_of(start, 16), half), :]


def attend(parts, outs, info, gain, w_in, gate_bias, w_out, bias, live):
    rows, cols, width = parts[0].shape
    heads, span = bias.shape[0], bias.shape[1]
    half = span // outs
    tile = 256 if span % 256 == 0 else span
    whole = lambda array: pl.BlockSpec(
        array.shape, lambda i, *_, nd=array.ndim: (0,) * nd, pipeline_mode=pl.Buffered(1)
    )
    shared = (gain, w_in, gate_bias, w_out, bias, live)
    grid_spec = pltpu.PrefetchScalarGridSpec(
        num_scalar_prefetch=1,
        grid=(rows,),
        in_specs=[pl.BlockSpec((1, cols, width), lambda i, *_: (i, 0, 0)) for _ in parts]
        + [whole(array) for array in shared],
        out_specs=[pl.BlockSpec((1, half, width), lambda i, *_: (i, 0, 0)) for _ in range(outs)],
        scratch_shapes=[
            pltpu.VMEM((heads, span, span), jnp.float32),
            pltpu.VMEM((span, width), jnp.bfloat16),
            pltpu.VMEM((span, width), jnp.bfloat16),
            pltpu.VMEM((span, 2 * width), jnp.bfloat16),
            pltpu.VMEM((span, width), jnp.float32),
            pltpu.VMEM((span, width), jnp.bfloat16),
        ],
    )
    return pl.pallas_call(
        functools.partial(attend_kernel, len(parts), heads, tile),
        grid_spec=grid_spec,
        out_shape=[jax.ShapeDtypeStruct((rows, half, width), jnp.bfloat16) for _ in range(outs)],
        compiler_params=pltpu.CompilerParams(vmem_limit_bytes=48 * 1024 * 1024),
        cost_estimate=pl.CostEstimate(
            flops=rows * heads * span * span * 256 * 4,
            bytes_accessed=rows * span * width * 4,
            transcendentals=rows * heads * span * span,
        ),
    )(info, *parts, *shared)


def per_device(
    n_col,
    n_head,
    pair,
    crop_length,
    residue_mask,
    ln_gain,
    w_query,
    w_key,
    w_value,
    w_gate,
    gate_bias,
    w_bias,
    w_out,
):
    rows_here, cols_here, width = pair.shape
    grid_len = residue_mask.shape[0]
    row_pos = lax.axis_index("row")
    col_pos = lax.axis_index("col")
    head_pos = lax.axis_index("head")
    places = n_col * n_head
    place = col_pos * n_head + head_pos
    own_rows = rows_here // places
    chunk = 8 if own_rows % 8 == 0 else own_rows
    chunks = own_rows // chunk

    def rows_of(target, index):
        start = (target * n_head + head_pos) * own_rows + index * chunk
        return lax.dynamic_slice_in_dim(pair, start, chunk, 0)

    arrived = []
    for index in range(chunks):
        parts = [rows_of(col_pos, index)]
        for step in range(1, n_col):
            swap = [(d, d ^ step) for d in range(n_col)]
            parts.append(lax.ppermute(rows_of(col_pos ^ step, index), "col", swap))
        arrived.append(parts)

    local_chan = w_query.shape[1]
    local_heads = w_bias.shape[1]
    gain = ln_gain.reshape(1, width)
    w_bias_all = lax.all_gather(w_bias.T, "head", axis=0, tiled=True).T
    weights = jnp.concatenate([w_query, w_key, w_value, w_gate], axis=1).astype(jnp.float32)
    extra = jnp.zeros((8, weights.shape[1]), jnp.float32)
    extra = lax.dynamic_update_slice(extra, gate_bias[None], (0, 0))
    packed = lax.all_gather(jnp.concatenate([weights, extra], axis=0), "head", axis=0)
    w_in = packed[:, :width].reshape(n_head, width, 4, local_chan)
    w_in = jnp.transpose(w_in, (1, 2, 0, 3)).reshape(width, -1).astype(jnp.bfloat16)
    gate_bias_all = packed[:, width, :local_chan].reshape(1, -1)

    bias_rows = rows_here // n_head
    bias = pair_bias(
        lax.dynamic_slice_in_dim(pair, head_pos * bias_rows, bias_rows, 0), gain, w_bias_all
    ).astype(jnp.bfloat16)
    bias = lax.all_gather(bias, "col", axis=2, tiled=True)
    bias = lax.all_gather(bias, ("row", "head"), axis=1, tiled=True)

    total_len = crop_length[0]
    key_ids = jnp.arange(grid_len, dtype=jnp.int32)
    live = ((residue_mask == 1) & (key_ids < total_len)).astype(jnp.int32).reshape(1, grid_len)

    update = jnp.zeros((places, own_rows, cols_here // n_head, width), jnp.bfloat16)
    for index in range(chunks):
        first_row = row_pos * rows_here + place * own_rows + index * chunk
        info = jnp.stack([col_pos, place, first_row, total_len]).astype(jnp.int32)
        outs = attend(arrived[index], places, info, gain, w_in, gate_bias_all, w_out, bias, live)
        for step in range(places):
            got = outs[step]
            if step > 0:
                swap = [(d, d ^ step) for d in range(places)]
                got = lax.ppermute(got, ("col", "head"), swap)
            update = lax.dynamic_update_slice(
                update, got[None], (place ^ step, index * chunk, 0, 0)
            )
    return update.reshape(rows_here, cols_here // n_head, width)


def solution(mesh):
    placed = (
        P(("parts", "row"), "col", None),
        P("parts"),
        P("parts"),
        P(),
        P(None, "head"),
        P(None, "head"),
        P(None, "head"),
        P(None, "head"),
        P("head"),
        P(None, "head"),
        P(),
    )
    return jax.shard_map(
        functools.partial(per_device, mesh.shape["col"], mesh.shape["head"]),
        mesh=mesh,
        in_specs=placed,
        out_specs=P(("parts", "row"), ("col", "head"), None),
        check_vma=False,
    )
```

time: 1140 us -> 479 us (0.42)
  waiting for transfers between devices: 426 us -> 100 us
  matrix products: 315 us -> 0 us
  Pallas kernels: 0 us -> 284 us
  other arithmetic: 200 us -> 1.46 us
  local copies, waits for them, and re-layouts: 174 us -> 43.9 us
  starting transfers between devices: 0.31 us -> 19.5 us
    all_gather x3 -> x1, waiting for transfers between devices: 376 us -> 24.2 us  [per_device(): bias = lax.all_gather(bias, ('row', 'head'), axis=1, tiled=True)]
    dot_general x54 -> x0, matrix products: 315 us -> none  [the longest x24 140 us: attend_tile(): jnp.einsum('bhjk,bkhd->bjhd', weights, v_tile, preferred_element_type=jnp...]
    pallas_call x0 -> x7, Pallas kernels: none -> 284 us  [the longest x6 268 us: attend(): pl.pallas_call(functools.partial(attend_kernel, len(parts), heads, tile),...]
    reduce_sum x27 -> x0, other arithmetic: 146 us -> none  [the longest x24 110 us: attend_tile(): total_w = jnp.sum(expo, axis=-1)]
    ppermute x0 -> x24, waiting for transfers between devices: none -> 76.2 us  [the longest x18 66.8 us: per_device(): got = lax.ppermute(got, ('col', 'head'), swap)]
    unnamed x27 -> x24, local copies, waits for them, and re-layouts: 54 us -> 1.64 us
    reduce_scatter x1 -> x0, waiting for transfers between devices: 49.4 us -> none  [per_device(): lax.psum_scatter(partial_terms, 'head', scatter_dimension=1, tiled=True)]
    all_gather x2 -> x0, local copies, waits for them, and re-layouts: 41.7 us -> none  [the longest x1 21.6 us: per_device(): lax.all_gather(keys_here, 'col', axis=1, tiled=True)]
  transfers between devices with their start and end apart: 4 -> 25, of which waited for: 3 -> 11; matrix products, arithmetic and copies ran while one was open for 11% -> 7% of each run, Pallas kernels for 0% -> 56%
where the time goes in v1:
time: 479 us; the launch traced here: 478 us
  Pallas kernels  284 us (59%)
  waiting for transfers between devices  100 us (21%)
  local copies, waits for them, and re-layouts  43.9 us (9%)
  starting transfers between devices  19.5 us (4%)
  blocking collectives  15 us (3%)
  between operations  14.4 us (3%)
    pallas_call x6, Pallas kernels, attend(): pl.pallas_call(functools.partial(attend_kernel, len(parts), heads, tile),...  268 us
    ppermute x18, waiting for transfers between devices, per_device(): got = lax.ppermute(got, ('col', 'head'), swap)  66.8 us
    all_gather x1, waiting for transfers between devices, per_device(): bias = lax.all_gather(bias, ('row', 'head'), axis=1, tiled=True)  24.2 us
    dynamic_update_slice x24, local copies, waits for them, and re-layouts, per_device(): lax.dynamic_update_slice(update, got[None], (place ^ step, index * chunk,...  18.6 us
    pallas_call x1, Pallas kernels, pair_bias(): pl.pallas_call(bias_kernel, grid=(rows // step,), in_specs=[pl.BlockSpec(...  16 us
    ppermute x18, starting transfers between devices, per_device(): got = lax.ppermute(got, ('col', 'head'), swap)  11.9 us
    all_gather x1, blocking collectives, per_device(): bias = lax.all_gather(bias, 'col', axis=2, tiled=True)  10.9 us
  transfers between devices with their start and end apart: 25, of which 11 were waited for; matrix products, arithmetic and copies ran while one was open for 7% of the time, Pallas kernels for 56%

profile of v1, /device:TPU:0, one launch (start us, length us, event | category | flops | bytes accessed | tf_op | source)
XLA Modules:
  0.0 478.4 jit_solution(4318620809647609677)
XLA Ops:
  6.5 2.0 all-gather.1
  9.2 8.6 %constant_dynamic-slice_fusion.10.pair_ref = bf16[96,384,128]{2,1,0:T(8,128)(2,1)} fusion(bf16[192,384,128]{2,1,0:T(8,128)(2,1)} %param.11, s32[]{:T(128)S(6)} %select_n.36), kind=kLoop, calls=%fused_computation.38 | loop fusion | bytes 18874372 | tf_op jit(solution)/shard_map/dynamic_slice | solution.py:203
  17.8 16.0 %shard_map.109 = f32[4,96,384]{2,1,0:T(8,128)} custom-call(bf16[96,384,128]{2,1,0:T(8,128)(2,1)} %constant_dynamic-slice_fusion.10.pair_ref, f32[1,128]{1,0:T(1,128)} %bitcast.70, bf16[8,128]{1,0:T(8,128)(2,1)} %dynamic_update_slice.79.w_ref), custom_call_target="tpu_custom_call" | custom-call | flops 75497472 | bytes 9437184 | tf_op jit(solution)/shard_map/pallas_call | solution.py:35
  34.9 10.9 %all_gather.18 = bf16[4,96,768]{2,1,0:T(8,128)(2,1)} all-gather(bf16[4,96,384]{2,1,0:T(8,128)(2,1)S(1)} %convert_element_type.18), channel_id=1, replica_groups=mesh['parts'=2,'row'=4,'col'=2,'head'=2] {'col'}, dimensions={2}, use_global_device_ids=true | all-gather | bytes 884736 | tf_op jit(solution)/shard_map/all_gather | solution.py:205
  46.0 6.5 %constant_dynamic-slice_fusion = (bf16[8,384,128]{2,1,0:T(8,128)(2,1)}, bf16[8,384,128]{2,1,0:T(8,128)(2,1)}, bf16[8,384,128]{2,1,0:T(8,128)(2,1)}, bf16[8,384,1...) fusion(bf16[192,384,128]{2,1,0:T(8,128)(2,1)} %param.11, ...), kind=kLoop, calls=%fused_computation.28 | loop fusion | bytes 18874416 | tf_op jit(solution)/shard_map/dynamic_slice | solution.py:179
  59.6 2.0 all-gather
  63.8 9.4 %collective-permute-done.20.refs_1_ = bf16[8,384,128]{2,1,0:T(8,128)(2,1)} collective-permute-done((bf16[8,384,128]{2,1,0:T(8,128)(2,1)}, bf16[8,384,128]{2,1,0:T(8,128)(2,1)}, u32[]{:S(2)}, u32[]{:S(2)}) %collective-permute-start.20) | collective-permute-done | bytes 786464 | tf_op jit(solution)/shard_map/ppermute | solution.py:186
  75.0 24.2 %all-gather.4.cloned.1.call-done.refs_6_ = bf16[4,768,768]{2,1,0:T(8,128)(2,1)} async-done(((bf16[4,96,768]{2,1,0:T(8,128)(2,1)}), bf16[4,768,768]{2,1,0:T(8,128)(2,1)}) %all-gather.4.cloned.1.call-update) | async-done | bytes 4718608 | tf_op jit(solution)/shard_map/all_gather | solution.py:206
  100.3 44.7 %shard_map.115 = (bf16[8,192,128]{2,1,0:T(8,128)(2,1)S(1)}, bf16[8,192,128]{2,1,0:T(8,128)(2,1)S(1)}, bf16[8,192,128]{2,1,0:T(8,128)(2,1)S(1)}, bf16[8,192,128]{2,1,0:T(8,128)(2,1)S(1)}) custom-call(s32[4]{0:T(128)S(1)} %get-tuple-element.53.info_ref, bf16[8,384,128]{2,1,0:T(8,128)(2,1)S(1)} %copy-done.1, ...), custom_call_target="tpu_custom_call" | custom-call | flops 19327352832 | bytes 3145728 | tf_op jit(solution)/shard_map/pallas_call | solution.py:138
  145.4 44.6 %shard_map.114 = (bf16[8,192,128]{2,1,0:T(8,128)(2,1)S(1)}, bf16[8,192,128]{2,1,0:T(8,128)(2,1)S(1)}, bf16[8,192,128]{2,1,0:T(8,128)(2,1)S(1)}, bf16[8,192,128]{2,1,0:T(8,128)(2,1)S(1)}) custom-call(s32[4]{0:T(128)S(1)} %get-tuple-element.67.info_ref, bf16[8,384,128]{2,1,0:T(8,128)(2,1)S(1)} %copy-done, ...), custom_call_target="tpu_custom_call" | custom-call | flops 19327352832 | bytes 3145728 | tf_op jit(solution)/shard_map/pallas_call | solution.py:138
  191.5 44.5 %shard_map.113 = (bf16[8,192,128]{2,1,0:T(8,128)(2,1)S(1)}, bf16[8,192,128]{2,1,0:T(8,128)(2,1)S(1)}, bf16[8,192,128]{2,1,0:T(8,128)(2,1)S(1)}, bf16[8,192,128]{2,1,0:T(8,128)(2,1)S(1)}) custom-call(s32[4]{0:T(128)S(1)} %get-tuple-element.68.info_ref, bf16[8,384,128]{2,1,0:T(8,128)(2,1)S(1)} %get-tuple-element.59.refs_0_, ...), custom_call_target="tpu_custom_call" | custom-call | flops 19327352832 | bytes 3145728 | tf_op jit(solution)/shard_map/pallas_call | solution.py:138
  236.3 44.5 %shard_map.110 = (bf16[8,192,128]{2,1,0:T(8,128)(2,1)S(1)}, bf16[8,192,128]{2,1,0:T(8,128)(2,1)S(1)}, bf16[8,192,128]{2,1,0:T(8,128)(2,1)S(1)}, bf16[8,192,128]{2,1,0:T(8,128)(2,1)S(1)}) custom-call(s32[4]{0:T(128)S(1)} %add_add_fusion.info_ref, bf16[8,384,128]{2,1,0:T(8,128)(2,1)S(1)} %get-tuple-element.65.refs_0_, ...), custom_call_target="tpu_custom_call" | custom-call | flops 19327352832 | bytes 3145728 | tf_op jit(solution)/shard_map/pallas_call | solution.py:138
  281.4 44.5 %shard_map.112 = (bf16[8,192,128]{2,1,0:T(8,128)(2,1)S(1)}, bf16[8,192,128]{2,1,0:T(8,128)(2,1)S(1)}, bf16[8,192,128]{2,1,0:T(8,128)(2,1)S(1)}, bf16[8,192,128]{2,1,0:T(8,128)(2,1)S(1)}) custom-call(s32[4]{0:T(128)S(1)} %get-tuple-element.69.info_ref, bf16[8,384,128]{2,1,0:T(8,128)(2,1)S(1)} %get-tuple-element.61.refs_0_, ...), custom_call_target="tpu_custom_call" | custom-call | flops 19327352832 | bytes 3145728 | tf_op jit(solution)/shard_map/pallas_call | solution.py:138
  327.5 44.8 %shard_map.111 = (bf16[8,192,128]{2,1,0:T(8,128)(2,1)S(1)}, bf16[8,192,128]{2,1,0:T(8,128)(2,1)S(1)}, bf16[8,192,128]{2,1,0:T(8,128)(2,1)S(1)}, bf16[8,192,128]{2,1,0:T(8,128)(2,1)S(1)}) custom-call(s32[4]{0:T(128)S(1)} %get-tuple-element.70.info_ref, bf16[8,384,128]{2,1,0:T(8,128)(2,1)S(1)} %get-tuple-element.63.refs_0_, ...), custom_call_target="tpu_custom_call" | custom-call | flops 19327352832 | bytes 3145728 | tf_op jit(solution)/shard_map/pallas_call | solution.py:138
  372.3 6.1 %broadcast_in_dim.80 = bf16[4,48,192,128]{3,2,1,0:T(8,128)(2,1)} broadcast(bf16[]{:T(256)} %constant.15.clone.1), dimensions={} | broadcast | bytes 9437186 | tf_op jit(solution)/shard_map/broadcast_in_dim | solution.py:212
  381.4 9.2 %collective-permute-done.3 = bf16[8,192,128]{2,1,0:T(8,128)(2,1)S(1)} collective-permute-done((bf16[8,192,128]{2,1,0:T(8,128)(2,1)S(1)}, bf16[8,192,128]{2,1,0:T(8,128)(2,1)S(1)}, u32[]{:S(2)}, u32[]{:S(2)}) %collective-permute-start.3) | collective-permute-done | bytes 393248 | tf_op jit(solution)/shard_map/ppermute | solution.py:221
  394.4 8.2 %collective-permute-done.6 = bf16[8,192,128]{2,1,0:T(8,128)(2,1)S(1)} collective-permute-done((bf16[8,192,128]{2,1,0:T(8,128)(2,1)S(1)}, bf16[8,192,128]{2,1,0:T(8,128)(2,1)S(1)}, u32[]{:S(2)}, u32[]{:S(2)}) %collective-permute-start.6) | collective-permute-done | bytes 393248 | tf_op jit(solution)/shard_map/ppermute | solution.py:221
  403.3 5.9 %collective-permute-done.7 = bf16[8,192,128]{2,1,0:T(8,128)(2,1)S(1)} collective-permute-done((bf16[8,192,128]{2,1,0:T(8,128)(2,1)S(1)}, bf16[8,192,128]{2,1,0:T(8,128)(2,1)S(1)}, u32[]{:S(2)}, u32[]{:S(2)}) %collective-permute-start.7) | collective-permute-done | bytes 393248 | tf_op jit(solution)/shard_map/ppermute | solution.py:221
  413.7 7.6 %collective-permute-done.10 = bf16[8,192,128]{2,1,0:T(8,128)(2,1)S(1)} collective-permute-done((bf16[8,192,128]{2,1,0:T(8,128)(2,1)S(1)}, bf16[8,192,128]{2,1,0:T(8,128)(2,1)S(1)}, u32[]{:S(2)}, u32[]{:S(2)}) %collective-permute-start.10) | collective-permute-done | bytes 393248 | tf_op jit(solution)/shard_map/ppermute | solution.py:221
  422.0 7.1 %collective-permute-done.11 = bf16[8,192,128]{2,1,0:T(8,128)(2,1)S(1)} collective-permute-done((bf16[8,192,128]{2,1,0:T(8,128)(2,1)S(1)}, bf16[8,192,128]{2,1,0:T(8,128)(2,1)S(1)}, u32[]{:S(2)}, u32[]{:S(2)}) %collective-permute-start.11) | collective-permute-done | bytes 393248 | tf_op jit(solution)/shard_map/ppermute | solution.py:221
  432.9 8.2 %collective-permute-done.14 = bf16[8,192,128]{2,1,0:T(8,128)(2,1)S(1)} collective-permute-done((bf16[8,192,128]{2,1,0:T(8,128)(2,1)S(1)}, bf16[8,192,128]{2,1,0:T(8,128)(2,1)S(1)}, u32[]{:S(2)}, u32[]{:S(2)}) %collective-permute-start.14) | collective-permute-done | bytes 393248 | tf_op jit(solution)/shard_map/ppermute | solution.py:221
  441.9 6.0 %collective-permute-done.15 = bf16[8,192,128]{2,1,0:T(8,128)(2,1)S(1)} collective-permute-done((bf16[8,192,128]{2,1,0:T(8,128)(2,1)S(1)}, bf16[8,192,128]{2,1,0:T(8,128)(2,1)S(1)}, u32[]{:S(2)}, u32[]{:S(2)}) %collective-permute-start.15) | collective-permute-done | bytes 393248 | tf_op jit(solution)/shard_map/ppermute | solution.py:221
  452.2 7.7 %collective-permute-done.18 = bf16[8,192,128]{2,1,0:T(8,128)(2,1)S(1)} collective-permute-done((bf16[8,192,128]{2,1,0:T(8,128)(2,1)S(1)}, bf16[8,192,128]{2,1,0:T(8,128)(2,1)S(1)}, u32[]{:S(2)}, u32[]{:S(2)}) %collective-permute-start.18) | collective-permute-done | bytes 393248 | tf_op jit(solution)/shard_map/ppermute | solution.py:221
  460.6 7.0 %collective-permute-done.19 = bf16[8,192,128]{2,1,0:T(8,128)(2,1)S(1)} collective-permute-done((bf16[8,192,128]{2,1,0:T(8,128)(2,1)S(1)}, bf16[8,192,128]{2,1,0:T(8,128)(2,1)S(1)}, u32[]{:S(2)}, u32[]{:S(2)}) %collective-permute-start.19) | collective-permute-done | bytes 393248 | tf_op jit(solution)/shard_map/ppermute | solution.py:221
  (103 shorter events, 43.7 us)
Async XLA Ops:
  6.5 92.6 %all-gather.4.cloned.1.call-start = ((), (), s32[]{:S(2)}) async-start(), calls=%async_computation | async-start | bytes 5308416 | tf_op jit(solution)/shard_map/all_gather | solution.py:206
  52.4 20.8 %collective-permute-start.20 = (bf16[8,384,128]{2,1,0:T(8,128)(2,1)}, bf16[8,384,128]{2,1,0:T(8,128)(2,1)}, u32[]{:S(2)}, u32[]{:S(2)}) collective-permute-start(bf16[8,384,128]{2,1,0:T(8,128)(2,1)} %get-tuple-element.55), channel_id=1, source_target_pairs={{0,2},{2,0},{1,3},{3,1},{4,6},{6,4},{5,7},{7,5},{8,10},{10,8},{9,1... | collective-permute-start | bytes 2359304 | tf_op jit(solution)/shard_map/ppermute | solution.py:186
  54.2 90.8 %collective-permute-start.16 = (bf16[8,384,128]{2,1,0:T(8,128)(2,1)}, bf16[8,384,128]{2,1,0:T(8,128)(2,1)}, u32[]{:S(2)}, u32[]{:S(2)}) collective-permute-start(bf16[8,384,128]{2,1,0:T(8,128)(2,1)} %get-tuple-element.56), channel_id=1, source_target_pairs={{0,2},{2,0},{1,3},{3,1},{4,6},{6,4},{5,7},{7,5},{8,10},{10,8},{9,1... | collective-permute-start | bytes 2359304 | tf_op jit(solution)/shard_map/ppermute | solution.py:186
  54.5 135.5 %collective-permute-start.12 = (bf16[8,384,128]{2,1,0:T(8,128)(2,1)}, bf16[8,384,128]{2,1,0:T(8,128)(2,1)}, u32[]{:S(2)}, u32[]{:S(2)}) collective-permute-start(bf16[8,384,128]{2,1,0:T(8,128)(2,1)} %get-tuple-element.58), channel_id=1, source_target_pairs={{0,2},{2,0},{1,3},{3,1},{4,6},{6,4},{5,7},{7,5},{8,10},{10,8},{9,1... | collective-permute-start | bytes 2359304 | tf_op jit(solution)/shard_map/ppermute | solution.py:186
  56.2 224.6 %collective-permute-start.8 = (bf16[8,384,128]{2,1,0:T(8,128)(2,1)}, bf16[8,384,128]{2,1,0:T(8,128)(2,1)}, u32[]{:S(2)}, u32[]{:S(2)}) collective-permute-start(bf16[8,384,128]{2,1,0:T(8,128)(2,1)} %get-tuple-element.60), channel_id=1, source_target_pairs={{0,2},{2,0},{1,3},{3,1},{4,6},{6,4},{5,7},{7,5},{8,10},{10,8},{9,1... | collective-permute-start | bytes 2359304 | tf_op jit(solution)/shard_map/ppermute | solution.py:186
  56.5 269.4 %collective-permute-start.4 = (bf16[8,384,128]{2,1,0:T(8,128)(2,1)}, bf16[8,384,128]{2,1,0:T(8,128)(2,1)}, u32[]{:S(2)}, u32[]{:S(2)}) collective-permute-start(bf16[8,384,128]{2,1,0:T(8,128)(2,1)} %get-tuple-element.62), channel_id=1, source_target_pairs={{0,2},{2,0},{1,3},{3,1},{4,6},{6,4},{5,7},{7,5},{8,10},{10,8},{9,1... | collective-permute-start | bytes 2359304 | tf_op jit(solution)/shard_map/ppermute | solution.py:186
  73.2 162.9 %collective-permute-start = (bf16[8,384,128]{2,1,0:T(8,128)(2,1)}, bf16[8,384,128]{2,1,0:T(8,128)(2,1)}, u32[]{:S(2)}, u32[]{:S(2)}) collective-permute-start(bf16[8,384,128]{2,1,0:T(8,128)(2,1)} %get-tuple-element.64), channel_id=1, source_target_pairs={{0,2},{2,0},{1,3},{3,1},{4,6},{6,4},{5,7},{7,5},{8,10},{10,8},{9,1... | collective-permute-start | bytes 2359304 | tf_op jit(solution)/shard_map/ppermute | solution.py:186
  145.1 324.1 %collective-permute-start.21 = (bf16[8,192,128]{2,1,0:T(8,128)(2,1)S(1)}, bf16[8,192,128]{2,1,0:T(8,128)(2,1)S(1)}, u32[]{:S(2)}, u32[]{:S(2)}) collective-permute-start(bf16[8,192,128]{2,1,0:T(8,128)(2,1)S(1)} %get-tuple-element.50), channel_id=1, source_target_pairs={{0,1},{1,0},{2,3},{3,2},{4,5},{5,4},{6,7},{7,6},{8,9},{9,8},{10,11... | collective-permute-start | bytes 1179656 | tf_op jit(solution)/shard_map/ppermute | solution.py:221
  189.9 280.0 %collective-permute-start.22 = (bf16[8,192,128]{2,1,0:T(8,128)(2,1)S(1)}, bf16[8,192,128]{2,1,0:T(8,128)(2,1)S(1)}, u32[]{:S(2)}, u32[]{:S(2)}) collective-permute-start(bf16[8,192,128]{2,1,0:T(8,128)(2,1)S(1)} %get-tuple-element.51), channel_id=1, source_target_pairs={{0,2},{1,3},{2,0},{3,1},{4,6},{5,7},{6,4},{7,5},{8,10},{9,11},{10,... | collective-permute-start | bytes 1179656 | tf_op jit(solution)/shard_map/ppermute | solution.py:221
  236.1 234.7 %collective-permute-start.23 = (bf16[8,192,128]{2,1,0:T(8,128)(2,1)S(1)}, bf16[8,192,128]{2,1,0:T(8,128)(2,1)S(1)}, u32[]{:S(2)}, u32[]{:S(2)}) collective-permute-start(bf16[8,192,128]{2,1,0:T(8,128)(2,1)S(1)} %get-tuple-element.52), channel_id=1, source_target_pairs={{0,3},{1,2},{2,1},{3,0},{4,7},{5,6},{6,5},{7,4},{8,11},{9,10},{10,... | collective-permute-start | bytes 1179656 | tf_op jit(solution)/shard_map/ppermute | solution.py:221
  280.8 98.4 %collective-permute-start.1 = (bf16[8,192,128]{2,1,0:T(8,128)(2,1)S(1)}, bf16[8,192,128]{2,1,0:T(8,128)(2,1)S(1)}, u32[]{:S(2)}, u32[]{:S(2)}) collective-permute-start(bf16[8,192,128]{2,1,0:T(8,128)(2,1)S(1)} %get-tuple-element.30), channel_id=1, source_target_pairs={{0,1},{1,0},{2,3},{3,2},{4,5},{5,4},{6,7},{7,6},{8,9},{9,8},{10,11... | collective-permute-start | bytes 1179656 | tf_op jit(solution)/shard_map/ppermute | solution.py:221
  325.9 54.0 %collective-permute-start.2 = (bf16[8,192,128]{2,1,0:T(8,128)(2,1)S(1)}, bf16[8,192,128]{2,1,0:T(8,128)(2,1)S(1)}, u32[]{:S(2)}, u32[]{:S(2)}) collective-permute-start(bf16[8,192,128]{2,1,0:T(8,128)(2,1)S(1)} %get-tuple-element.31), channel_id=1, source_target_pairs={{0,2},{1,3},{2,0},{3,1},{4,6},{5,7},{6,4},{7,5},{8,10},{9,11},{10,... | collective-permute-start | bytes 1179656 | tf_op jit(solution)/shard_map/ppermute | solution.py:221
  379.2 11.4 %collective-permute-start.3 = (bf16[8,192,128]{2,1,0:T(8,128)(2,1)S(1)}, bf16[8,192,128]{2,1,0:T(8,128)(2,1)S(1)}, u32[]{:S(2)}, u32[]{:S(2)}) collective-permute-start(bf16[8,192,128]{2,1,0:T(8,128)(2,1)S(1)} %get-tuple-element.32), channel_id=1, source_target_pairs={{0,3},{1,2},{2,1},{3,0},{4,7},{5,6},{6,5},{7,4},{8,11},{9,10},{10,... | collective-permute-start | bytes 1179656 | tf_op jit(solution)/shard_map/ppermute | solution.py:221
  380.0 12.7 %collective-permute-start.5 = (bf16[8,192,128]{2,1,0:T(8,128)(2,1)S(1)}, bf16[8,192,128]{2,1,0:T(8,128)(2,1)S(1)}, u32[]{:S(2)}, u32[]{:S(2)}) collective-permute-start(bf16[8,192,128]{2,1,0:T(8,128)(2,1)S(1)} %get-tuple-element.34), channel_id=1, source_target_pairs={{0,1},{1,0},{2,3},{3,2},{4,5},{5,4},{6,7},{7,6},{8,9},{9,8},{10,11... | collective-permute-start | bytes 1179656 | tf_op jit(solution)/shard_map/ppermute | solution.py:221
  390.6 12.0 %collective-permute-start.6 = (bf16[8,192,128]{2,1,0:T(8,128)(2,1)S(1)}, bf16[8,192,128]{2,1,0:T(8,128)(2,1)S(1)}, u32[]{:S(2)}, u32[]{:S(2)}) collective-permute-start(bf16[8,192,128]{2,1,0:T(8,128)(2,1)S(1)} %get-tuple-element.35), channel_id=1, source_target_pairs={{0,2},{1,3},{2,0},{3,1},{4,6},{5,7},{6,4},{7,5},{8,10},{9,11},{10,... | collective-permute-start | bytes 1179656 | tf_op jit(solution)/shard_map/ppermute | solution.py:221
  392.6 16.6 %collective-permute-start.7 = (bf16[8,192,128]{2,1,0:T(8,128)(2,1)S(1)}, bf16[8,192,128]{2,1,0:T(8,128)(2,1)S(1)}, u32[]{:S(2)}, u32[]{:S(2)}) collective-permute-start(bf16[8,192,128]{2,1,0:T(8,128)(2,1)S(1)} %get-tuple-element.36), channel_id=1, source_target_pairs={{0,3},{1,2},{2,1},{3,0},{4,7},{5,6},{6,5},{7,4},{8,11},{9,10},{10,... | collective-permute-start | bytes 1179656 | tf_op jit(solution)/shard_map/ppermute | solution.py:221
  409.3 12.0 %collective-permute-start.10 = (bf16[8,192,128]{2,1,0:T(8,128)(2,1)S(1)}, bf16[8,192,128]{2,1,0:T(8,128)(2,1)S(1)}, u32[]{:S(2)}, u32[]{:S(2)}) collective-permute-start(bf16[8,192,128]{2,1,0:T(8,128)(2,1)S(1)} %get-tuple-element.39), channel_id=1, source_target_pairs={{0,2},{1,3},{2,0},{3,1},{4,6},{5,7},{6,4},{7,5},{8,10},{9,11},{10,... | collective-permute-start | bytes 1179656 | tf_op jit(solution)/shard_map/ppermute | solution.py:221
  411.4 17.7 %collective-permute-start.11 = (bf16[8,192,128]{2,1,0:T(8,128)(2,1)S(1)}, bf16[8,192,128]{2,1,0:T(8,128)(2,1)S(1)}, u32[]{:S(2)}, u32[]{:S(2)}) collective-permute-start(bf16[8,192,128]{2,1,0:T(8,128)(2,1)S(1)} %get-tuple-element.40), channel_id=1, source_target_pairs={{0,3},{1,2},{2,1},{3,0},{4,7},{5,6},{6,5},{7,4},{8,11},{9,10},{10,... | collective-permute-start | bytes 1179656 | tf_op jit(solution)/shard_map/ppermute | solution.py:221
  421.3 9.9 %collective-permute-start.13 = (bf16[8,192,128]{2,1,0:T(8,128)(2,1)S(1)}, bf16[8,192,128]{2,1,0:T(8,128)(2,1)S(1)}, u32[]{:S(2)}, u32[]{:S(2)}) collective-permute-start(bf16[8,192,128]{2,1,0:T(8,128)(2,1)S(1)} %get-tuple-element.42), channel_id=1, source_target_pairs={{0,1},{1,0},{2,3},{3,2},{4,5},{5,4},{6,7},{7,6},{8,9},{9,8},{10,11... | collective-permute-start | bytes 1179656 | tf_op jit(solution)/shard_map/ppermute | solution.py:221
  429.1 12.0 %collective-permute-start.14 = (bf16[8,192,128]{2,1,0:T(8,128)(2,1)S(1)}, bf16[8,192,128]{2,1,0:T(8,128)(2,1)S(1)}, u32[]{:S(2)}, u32[]{:S(2)}) collective-permute-start(bf16[8,192,128]{2,1,0:T(8,128)(2,1)S(1)} %get-tuple-element.43), channel_id=1, source_target_pairs={{0,2},{1,3},{2,0},{3,1},{4,6},{5,7},{6,4},{7,5},{8,10},{9,11},{10,... | collective-permute-start | bytes 1179656 | tf_op jit(solution)/shard_map/ppermute | solution.py:221
  431.2 16.7 %collective-permute-start.15 = (bf16[8,192,128]{2,1,0:T(8,128)(2,1)S(1)}, bf16[8,192,128]{2,1,0:T(8,128)(2,1)S(1)}, u32[]{:S(2)}, u32[]{:S(2)}) collective-permute-start(bf16[8,192,128]{2,1,0:T(8,128)(2,1)S(1)} %get-tuple-element.44), channel_id=1, source_target_pairs={{0,3},{1,2},{2,1},{3,0},{4,7},{5,6},{6,5},{7,4},{8,11},{9,10},{10,... | collective-permute-start | bytes 1179656 | tf_op jit(solution)/shard_map/ppermute | solution.py:221
  441.1 8.9 %collective-permute-start.17 = (bf16[8,192,128]{2,1,0:T(8,128)(2,1)S(1)}, bf16[8,192,128]{2,1,0:T(8,128)(2,1)S(1)}, u32[]{:S(2)}, u32[]{:S(2)}) collective-permute-start(bf16[8,192,128]{2,1,0:T(8,128)(2,1)S(1)} %get-tuple-element.46), channel_id=1, source_target_pairs={{0,1},{1,0},{2,3},{3,2},{4,5},{5,4},{6,7},{7,6},{8,9},{9,8},{10,11... | collective-permute-start | bytes 1179656 | tf_op jit(solution)/shard_map/ppermute | solution.py:221
  447.8 12.0 %collective-permute-start.18 = (bf16[8,192,128]{2,1,0:T(8,128)(2,1)S(1)}, bf16[8,192,128]{2,1,0:T(8,128)(2,1)S(1)}, u32[]{:S(2)}, u32[]{:S(2)}) collective-permute-start(bf16[8,192,128]{2,1,0:T(8,128)(2,1)S(1)} %get-tuple-element.47), channel_id=1, source_target_pairs={{0,2},{1,3},{2,0},{3,1},{4,6},{5,7},{6,4},{7,5},{8,10},{9,11},{10,... | collective-permute-start | bytes 1179656 | tf_op jit(solution)/shard_map/ppermute | solution.py:221
  449.9 17.7 %collective-permute-start.19 = (bf16[8,192,128]{2,1,0:T(8,128)(2,1)S(1)}, bf16[8,192,128]{2,1,0:T(8,128)(2,1)S(1)}, u32[]{:S(2)}, u32[]{:S(2)}) collective-permute-start(bf16[8,192,128]{2,1,0:T(8,128)(2,1)S(1)} %get-tuple-element.48), channel_id=1, source_target_pairs={{0,3},{1,2},{2,1},{3,0},{4,7},{5,6},{6,5},{7,4},{8,11},{9,10},{10,... | collective-permute-start | bytes 1179656 | tf_op jit(solution)/shard_map/ppermute | solution.py:221
  (11 other events, 241.5 us)
Sparse Core Ops, SparseCore 0:
  45.9 53.1 all-gather.3

commit v2 on v1

--- a/solution.py
+++ b/solution.py
@@ -18,7 +18,7 @@
     return (centre * lax.rsqrt(spread + 1e-05) * gain).astype(jnp.bfloat16)
 
 
-def bias_kernel(pair_ref, gain_ref, w_ref, out_ref):
+def bias_kernel(first_ref, pair_ref, gain_ref, w_ref, out_ref):
     heads = out_ref.shape[0]
     for row in range(pair_ref.shape[0]):
         normed = layer_norm(pair_ref[row], gain_ref[...])
@@ -26,33 +26,37 @@
         out_ref[:, row, :] = plane[:heads]
 
 
-def pair_bias(pair, gain, w_bias):
-    rows, cols, width = pair.shape
+def pair_bias(pair, first, rows, gain, w_bias):
+    cols, width = pair.shape[1:]
     heads = w_bias.shape[1]
     padded = jnp.zeros((8 * pl.cdiv(heads, 8), width), jnp.bfloat16)
     padded = lax.dynamic_update_slice(padded, w_bias.T, (0, 0))
     step = 8
     return pl.pallas_call(
         bias_kernel,
-        grid=(rows // step,),
-        in_specs=[
-            pl.BlockSpec((step, cols, width), lambda i: (i, 0, 0)),
-            pl.BlockSpec((1, width), lambda i: (0, 0)),
-            pl.BlockSpec(padded.shape, lambda i: (0, 0)),
-        ],
-        out_specs=pl.BlockSpec((heads, step, cols), lambda i: (0, i, 0)),
+        grid_spec=pltpu.PrefetchScalarGridSpec(
+            num_scalar_prefetch=1,
+            grid=(rows // step,),
+            in_specs=[
+                pl.BlockSpec((step, cols, width), lambda i, first: (first[0] + i, 0, 0)),
+                pl.BlockSpec((1, width), lambda i, first: (0, 0)),
+                pl.BlockSpec(padded.shape, lambda i, first: (0, 0)),
+            ],
+            out_specs=pl.BlockSpec((heads, step, cols), lambda i, first: (0, i, 0)),
+        ),
         out_shape=jax.ShapeDtypeStruct((heads, rows, cols), jnp.float32),
         cost_estimate=pl.CostEstimate(
             flops=2 * rows * cols * width * 8, bytes_accessed=rows * cols * width * 2, transcendentals=0
         ),
-    )(pair, gain, padded)
+    )((first // step).reshape(1).astype(jnp.int32), pair, gain, padded)
 
 
 def attend_kernel(blocks, heads, tile, info_ref, *refs):
     pair_refs = refs[:blocks]
-    gain_ref, w_in_ref, gate_bias_ref, w_out_ref, bias_ref, live_ref = refs[blocks : blocks + 6]
-    rest = refs[blocks + 6 :]
-    out_refs, (bias_all, query_all, keys_all, values_all, gate_all, update_all) = rest[:-6], rest[-6:]
+    gain_ref, w_in_ref, gate_bias_ref, w_out_ref, bias_ref = refs[blocks : blocks + 5]
+    rest = refs[blocks + 5 :]
+    out_refs, scratch = rest[:-6], rest[-6:]
+    query_all, keys_all, keys_turned, values_all, gate_all, update_all = scratch
     span, width = keys_all.shape
     cols = pair_refs[0].shape[1]
     head_size = width // heads
@@ -62,16 +66,6 @@
 
     @pl.when(pl.program_id(0) == 0)
     def _():
-        live = live_ref[...] > 0
-        for head in range(heads):
-
-            @pl.loop(0, span // 64)
-            def _(part):
-                rows = pl.ds(pl.multiple_of(part * 64, 64), 64)
-                bias_all[head, rows, :] = jnp.where(
-                    live, bias_ref[head, rows, :].astype(jnp.float32), -1000000000.0
-                )
-
         values_all[:, width:] = jnp.ones((span, width), jnp.bfloat16)
 
     for step in range(blocks):
@@ -84,6 +78,7 @@
         values_all[rows, :width] = mixed[:, 2 * width : 3 * width].astype(jnp.bfloat16)
         gate_all[rows, :] = jax.nn.sigmoid(mixed[:, 3 * width :] + gate_bias_ref[...])
 
+    keys_turned[...] = keys_all[...].T
     lanes = lax.broadcasted_iota(jnp.int32, (1, width), 1) // head_size
     row_scale = (row_id < total_len).astype(jnp.float32)
 
@@ -94,8 +89,8 @@
         attended = jnp.zeros((tile, width), jnp.float32)
         for head in range(heads):
             masked = jnp.where(lanes == head, query, jnp.zeros_like(query))
-            scores = lax.dot_general(masked, keys_all[...], NT, preferred_element_type=jnp.float32)
-            scores = scores + bias_all[head, rows, :]
+            scores = jnp.dot(masked, keys_turned[...], preferred_element_type=jnp.float32)
+            scores = scores + bias_ref[head, rows, :].astype(jnp.float32)
             top = jnp.max(scores, axis=-1, keepdims=True)
             weights = jnp.exp(scores - top).astype(jnp.bfloat16)
             summed = jnp.dot(weights, values_all[...], preferred_element_type=jnp.float32)
@@ -111,15 +106,15 @@
         out_refs[step][0] = update_all[pl.ds(pl.multiple_of(start, 16), half), :]
 
 
-def attend(parts, outs, info, gain, w_in, gate_bias, w_out, bias, live):
+def attend(parts, outs, info, gain, w_in, gate_bias, w_out, bias):
     rows, cols, width = parts[0].shape
     heads, span = bias.shape[0], bias.shape[1]
     half = span // outs
-    tile = 256 if span % 256 == 0 else span
+    tile = span
     whole = lambda array: pl.BlockSpec(
         array.shape, lambda i, *_, nd=array.ndim: (0,) * nd, pipeline_mode=pl.Buffered(1)
     )
-    shared = (gain, w_in, gate_bias, w_out, bias, live)
+    shared = (gain, w_in, gate_bias, w_out, bias)
     grid_spec = pltpu.PrefetchScalarGridSpec(
         num_scalar_prefetch=1,
         grid=(rows,),
@@ -127,9 +122,9 @@
         + [whole(array) for array in shared],
         out_specs=[pl.BlockSpec((1, half, width), lambda i, *_: (i, 0, 0)) for _ in range(outs)],
         scratch_shapes=[
-            pltpu.VMEM((heads, span, span), jnp.float32),
             pltpu.VMEM((span, width), jnp.bfloat16),
             pltpu.VMEM((span, width), jnp.bfloat16),
+            pltpu.VMEM((width, span), jnp.bfloat16),
             pltpu.VMEM((span, 2 * width), jnp.bfloat16),
             pltpu.VMEM((span, width), jnp.float32),
             pltpu.VMEM((span, width), jnp.bfloat16),
@@ -178,14 +173,9 @@
         start = (target * n_head + head_pos) * own_rows + index * chunk
         return lax.dynamic_slice_in_dim(pair, start, chunk, 0)
 
-    arrived = []
-    for index in range(chunks):
-        parts = [rows_of(col_pos, index)]
-        for step in range(1, n_col):
-            swap = [(d, d ^ step) for d in range(n_col)]
-            parts.append(lax.ppermute(rows_of(col_pos ^ step, index), "col", swap))
-        arrived.append(parts)
-
+    first_parts = [
+        [rows_of(col_pos ^ step, index) for step in range(n_col)] for index in range(min(chunks, 2))
+    ]
     local_chan = w_query.shape[1]
     local_heads = w_bias.shape[1]
     gain = ln_gain.reshape(1, width)
@@ -199,28 +189,48 @@
     gate_bias_all = packed[:, width, :local_chan].reshape(1, -1)
 
     bias_rows = rows_here // n_head
-    bias = pair_bias(
-        lax.dynamic_slice_in_dim(pair, head_pos * bias_rows, bias_rows, 0), gain, w_bias_all
-    ).astype(jnp.bfloat16)
-    bias = lax.all_gather(bias, "col", axis=2, tiled=True)
+    first_row = head_pos * bias_rows
+    first_row, first_parts = lax.optimization_barrier((first_row, first_parts))
+    bias = pair_bias(pair, first_row, bias_rows, gain, w_bias_all)
+    arrived = []
+    for index in range(chunks):
+        if index < len(first_parts):
+            parts = first_parts[index]
+        else:
+            parts = [rows_of(col_pos ^ step, index) for step in range(n_col)]
+        for step in range(1, n_col):
+            swap = [(d, d ^ step) for d in range(n_col)]
+            parts[step] = lax.ppermute(parts[step], "col", swap)
+        arrived.append(parts)
+    bias = lax.all_gather(bias.astype(jnp.bfloat16), "col", axis=2, tiled=True)
+    bias, arrived[0] = lax.optimization_barrier((bias, arrived[0]))
     bias = lax.all_gather(bias, ("row", "head"), axis=1, tiled=True)
-
+    for index in range(1, min(chunks, 2)):
+        bias, arrived[index] = lax.optimization_barrier((bias, arrived[index]))
     total_len = crop_length[0]
     key_ids = jnp.arange(grid_len, dtype=jnp.int32)
-    live = ((residue_mask == 1) & (key_ids < total_len)).astype(jnp.int32).reshape(1, grid_len)
+    live = (residue_mask == 1) & (key_ids < total_len)
+    bias = jnp.where(live[None, None], bias, jnp.bfloat16(-1e9))
 
     update = jnp.zeros((places, own_rows, cols_here // n_head, width), jnp.bfloat16)
+    sent = [()] * chunks
     for index in range(chunks):
         first_row = row_pos * rows_here + place * own_rows + index * chunk
         info = jnp.stack([col_pos, place, first_row, total_len]).astype(jnp.int32)
-        outs = attend(arrived[index], places, info, gain, w_in, gate_bias_all, w_out, bias, live)
+        if index == 1:
+            info, arrived[2:] = lax.optimization_barrier((info, arrived[2:]))
+        if index >= 2:
+            info, sent[index - 2] = lax.optimization_barrier((info, sent[index - 2]))
+        outs = attend(arrived[index], places, info, gain, w_in, gate_bias_all, w_out, bias)
+        got = [outs[0]]
+        for step in range(1, places):
+            swap = [(d, d ^ step) for d in range(places)]
+            got.append(lax.ppermute(outs[step], ("col", "head"), swap))
+        sent[index] = tuple(got)
+    for index in range(chunks):
         for step in range(places):
-            got = outs[step]
-            if step > 0:
-                swap = [(d, d ^ step) for d in range(places)]
-                got = lax.ppermute(got, ("col", "head"), swap)
             update = lax.dynamic_update_slice(
-                update, got[None], (place ^ step, index * chunk, 0, 0)
+                update, sent[index][step][None], (place ^ step, index * chunk, 0, 0)
             )
     return update.reshape(rows_here, cols_here // n_head, width)
 

time: 479 us -> 429 us (0.90)
  Pallas kernels: 284 us -> 248 us
  local copies, waits for them, and re-layouts: 43.9 us -> 23.7 us
  other arithmetic: 1.46 us -> 6.47 us
    pallas_call x6, Pallas kernels: 268 us -> 232 us  [attend(): pl.pallas_call(functools.partial(attend_kernel, len(parts), heads, tile),...]
    ppermute x24, waiting for transfers between devices: 76.2 us -> 101 us  [the longest x6 76.5 us: per_device(): parts[step] = lax.ppermute(parts[step], 'col', swap)]
    all_gather x1, waiting for transfers between devices: 24.2 us -> 0.01 us  [per_device(): bias = lax.all_gather(bias, ('row', 'head'), axis=1, tiled=True)]
    dynamic_update_slice x24, local copies, waits for them, and re-layouts: 18.6 us -> 7.33 us  [per_device(): lax.dynamic_update_slice(update, sent[index][step][None], (place ^ step,...]
    dynamic_slice x1 -> x0, local copies, waits for them, and re-layouts: 8.6 us -> none  [per_device(): lax.dynamic_slice_in_dim(pair, head_pos * bias_rows, bias_rows, 0)]
    select_n x0 -> x1, other arithmetic: none -> 5 us  [per_device(): bias = jnp.where(live[None, None], bias, jnp.bfloat16(-1000000000.0))]
  transfers between devices with their start and end apart: 25 -> 25, of which waited for: 11 -> 9; matrix products, arithmetic and copies ran while one was open for 7% -> 3% of each run, Pallas kernels for 56% -> 40%
where the time goes in v2:
time: 429 us; the launch traced here: 428 us
  Pallas kernels  248 us (58%)
  waiting for transfers between devices  101 us (24%)
  local copies, waits for them, and re-layouts  23.7 us (6%)
  starting transfers between devices  20 us (5%)
  between operations  14.7 us (3%)
  blocking collectives  13.8 us (3%)
  other arithmetic  6.47 us (2%)
    pallas_call x6, Pallas kernels, attend(): pl.pallas_call(functools.partial(attend_kernel, len(parts), heads, tile),...  232 us
    ppermute x6, waiting for transfers between devices, per_device(): parts[step] = lax.ppermute(parts[step], 'col', swap)  76.5 us
    ppermute x18, waiting for transfers between devices, per_device(): got.append(lax.ppermute(outs[step], ('col', 'head'), swap))  24.4 us
    pallas_call x1, Pallas kernels, pair_bias(): pl.pallas_call(bias_kernel, grid_spec=pltpu.PrefetchScalarGridSpec(num_sc...  16 us
    ppermute x18, starting transfers between devices, per_device(): got.append(lax.ppermute(outs[step], ('col', 'head'), swap))  12.7 us
    all_gather x1, blocking collectives, per_device(): bias = lax.all_gather(bias.astype(jnp.bfloat16), 'col', axis=2, tiled=True)  9.9 us
  transfers between devices with their start and end apart: 25, of which 9 were waited for; matrix products, arithmetic and copies ran while one was open for 3% of the time, Pallas kernels for 40%

profile of v2, /device:TPU:0, one launch (start us, length us, event | category | flops | bytes accessed | tf_op | source)
XLA Modules:
  0.0 428.2 jit_solution(10744670794545166950)
XLA Ops:
  6.5 6.4 %constant_dynamic-slice_fusion = (bf16[8,384,128]{2,1,0:T(8,128)(2,1)}, bf16[8,384,128]{2,1,0:T(8,128)(2,1)}, bf16[8,384,128]{2,1,0:T(8,128)(2,1)S(1)}, bf16[8,3...) fusion(bf16[192,384,128]{2,1,0:T(8,128)(2,1)} %pair_ref.1, ...), kind=kLoop, calls=%fused_computation.29 | loop fusion | bytes 18874416 | tf_op jit(solution)/shard_map/dynamic_slice | solution.py:174
  13.0 2.9 collective-permute-start
  18.3 16.0 %shard_map.109 = f32[4,96,384]{2,1,0:T(8,128)} custom-call(s32[1]{0:T(128)} %bitcast.4.first_ref, bf16[192,384,128]{2,1,0:T(8,128)(2,1)} %pair_ref.1, f32[1,128]{1,0:T(1,128)} %bitcast.71, bf16[8,128]{1,0:T(8,128)(2,1)} %dynamic_update_slice.78.w_ref), custom_call_target="tpu_custom_call" | custom-call | flops 75497472 | bytes 9437184 | tf_op jit(solution)/shard_map/pallas_call | solution.py:35
  35.4 9.9 %all_gather.16 = bf16[4,96,768]{2,1,0:T(8,128)(2,1)} all-gather(bf16[4,96,384]{2,1,0:T(8,128)(2,1)S(1)} %convert_element_type.13), channel_id=1, replica_groups=mesh['parts'=2,'row'=4,'col'=2,'head'=2] {'col'}, dimensions={2}, use_global_device_ids=true | all-gather | bytes 884736 | tf_op jit(solution)/shard_map/all_gather | solution.py:205
  45.7 1.8 collective-permute-start.6
  50.4 2.2 all-gather
  55.5 10.7 %collective-permute-done.5.refs_1_ = bf16[8,384,128]{2,1,0:T(8,128)(2,1)} collective-permute-done((bf16[8,384,128]{2,1,0:T(8,128)(2,1)}, bf16[8,384,128]{2,1,0:T(8,128)(2,1)}, u32[]{:S(2)}, u32[]{:S(2)}) %collective-permute-start.5) | collective-permute-done | bytes 786464 | tf_op jit(solution)/shard_map/ppermute | solution.py:203
  66.2 16.9 %collective-permute-done.6.refs_1_ = bf16[8,384,128]{2,1,0:T(8,128)(2,1)} collective-permute-done((bf16[8,384,128]{2,1,0:T(8,128)(2,1)}, bf16[8,384,128]{2,1,0:T(8,128)(2,1)}, u32[]{:S(2)}, u32[]{:S(2)}) %collective-permute-start.6) | collective-permute-done | bytes 786464 | tf_op jit(solution)/shard_map/ppermute | solution.py:203
  83.1 16.9 %collective-permute-done.7.refs_1_ = bf16[8,384,128]{2,1,0:T(8,128)(2,1)} collective-permute-done((bf16[8,384,128]{2,1,0:T(8,128)(2,1)}, bf16[8,384,128]{2,1,0:T(8,128)(2,1)}, u32[]{:S(2)}, u32[]{:S(2)}) %collective-permute-start.7) | collective-permute-done | bytes 786464 | tf_op jit(solution)/shard_map/ppermute | solution.py:203
  99.9 16.9 %collective-permute-done.8.refs_1_ = bf16[8,384,128]{2,1,0:T(8,128)(2,1)} collective-permute-done((bf16[8,384,128]{2,1,0:T(8,128)(2,1)}, bf16[8,384,128]{2,1,0:T(8,128)(2,1)}, u32[]{:S(2)}, u32[]{:S(2)}) %collective-permute-start.8) | collective-permute-done | bytes 786464 | tf_op jit(solution)/shard_map/ppermute | solution.py:203
  116.8 15.2 %collective-permute-done.1.refs_1_ = bf16[8,384,128]{2,1,0:T(8,128)(2,1)} collective-permute-done((bf16[8,384,128]{2,1,0:T(8,128)(2,1)}, bf16[8,384,128]{2,1,0:T(8,128)(2,1)}, u32[]{:S(2)}, u32[]{:S(2)}) %collective-permute-start.1) | collective-permute-done | bytes 786464 | tf_op jit(solution)/shard_map/ppermute | solution.py:203
  132.0 5.0 %broadcast_select_fusion.refs_6_ = bf16[4,768,768]{2,1,0:T(8,128)(2,1)} fusion(bf16[4,768,768]{2,1,0:T(8,128)(2,1)} %all-gather.4.cloned.1.call-done, pred[768]{0:T(1024)(128)(4,1)S(1)} %fusion), kind=kLoop, calls=%fused_computation | loop fusion | flops 2359296 | bytes 9437952 | tf_op jit(solution)/shard_map/jit(_where)/select_n | solution.py:213
  137.0 38.7 %shard_map.111 = (bf16[8,192,128]{2,1,0:T(8,128)(2,1)S(1)}, bf16[8,192,128]{2,1,0:T(8,128)(2,1)S(1)}, bf16[8,192,128]{2,1,0:T(8,128)(2,1)S(1)}, bf16[8,192,128]{2,1,0:T(8,128)(2,1)S(1)}) custom-call(s32[4]{0:T(128)S(1)} %get-tuple-element.86.info_ref, bf16[8,384,128]{2,1,0:T(8,128)(2,1)S(1)} %copy-done.1, ...), custom_call_target="tpu_custom_call" | custom-call | flops 19327352832 | bytes 3145728 | tf_op jit(solution)/shard_map/pallas_call | solution.py:133
  177.9 38.7 %shard_map.110 = (bf16[8,192,128]{2,1,0:T(8,128)(2,1)S(1)}, bf16[8,192,128]{2,1,0:T(8,128)(2,1)S(1)}, bf16[8,192,128]{2,1,0:T(8,128)(2,1)S(1)}, bf16[8,192,128]{2,1,0:T(8,128)(2,1)S(1)}) custom-call(s32[4]{0:T(128)S(1)} %get-tuple-element.150.info_ref, bf16[8,384,128]{2,1,0:T(8,128)(2,1)S(1)} %copy-done, bf16[8,384,128]{2,1,0:T(8,128)(2,1)} %collective-permute-done.refs_1_, ...), custom_call_target="tpu_custom_call" | custom-call | flops 19327352832 | bytes 3145728 | tf_op jit(solution)/shard_map/pallas_call | solution.py:133
  218.6 38.9 %shard_map.113 = (bf16[8,192,128]{2,1,0:T(8,128)(2,1)S(1)}, bf16[8,192,128]{2,1,0:T(8,128)(2,1)S(1)}, bf16[8,192,128]{2,1,0:T(8,128)(2,1)S(1)}, bf16[8,192,128]{2,1,0:T(8,128)(2,1)S(1)}) custom-call(s32[4]{0:T(128)S(1)} %get-tuple-element.108.info_ref, bf16[8,384,128]{2,1,0:T(8,128)(2,1)S(1)} %get-tuple-element.109.refs_0_, ...), custom_call_target="tpu_custom_call" | custom-call | flops 19327352832 | bytes 3145728 | tf_op jit(solution)/shard_map/pallas_call | solution.py:133
  259.4 38.7 %shard_map.112 = (bf16[8,192,128]{2,1,0:T(8,128)(2,1)S(1)}, bf16[8,192,128]{2,1,0:T(8,128)(2,1)S(1)}, bf16[8,192,128]{2,1,0:T(8,128)(2,1)S(1)}, bf16[8,192,128]{2,1,0:T(8,128)(2,1)S(1)}) custom-call(s32[4]{0:T(128)S(1)} %add_add_fusion.info_ref, bf16[8,384,128]{2,1,0:T(8,128)(2,1)S(1)} %get-tuple-element.98.refs_0_, ...), custom_call_target="tpu_custom_call" | custom-call | flops 19327352832 | bytes 3145728 | tf_op jit(solution)/shard_map/pallas_call | solution.py:133
  299.4 2.4 broadcast_in_dim.93
  303.4 7.5 %collective-permute-done.13 = bf16[8,192,128]{2,1,0:T(8,128)(2,1)S(1)} collective-permute-done((bf16[8,192,128]{2,1,0:T(8,128)(2,1)S(1)}, bf16[8,192,128]{2,1,0:T(8,128)(2,1)S(1)}, u32[]{:S(2)}, u32[]{:S(2)}) %collective-permute-start.13) | collective-permute-done | bytes 393248 | tf_op jit(solution)/shard_map/ppermute | solution.py:228
  310.9 6.7 %collective-permute-done.14 = bf16[8,192,128]{2,1,0:T(8,128)(2,1)S(1)} collective-permute-done((bf16[8,192,128]{2,1,0:T(8,128)(2,1)S(1)}, bf16[8,192,128]{2,1,0:T(8,128)(2,1)S(1)}, u32[]{:S(2)}, u32[]{:S(2)}) %collective-permute-start.14) | collective-permute-done | bytes 393248 | tf_op jit(solution)/shard_map/ppermute | solution.py:228
  318.3 38.9 %shard_map.114 = (bf16[8,192,128]{2,1,0:T(8,128)(2,1)S(1)}, bf16[8,192,128]{2,1,0:T(8,128)(2,1)S(1)}, bf16[8,192,128]{2,1,0:T(8,128)(2,1)S(1)}, bf16[8,192,128]{2,1,0:T(8,128)(2,1)S(1)}) custom-call(s32[4]{0:T(128)S(1)} %get-tuple-element.119.info_ref, bf16[8,384,128]{2,1,0:T(8,128)(2,1)S(1)} %get-tuple-element.120.refs_0_, ...), custom_call_target="tpu_custom_call" | custom-call | flops 19327352832 | bytes 3145728 | tf_op jit(solution)/shard_map/pallas_call | solution.py:133
  359.4 38.7 %shard_map.115 = (bf16[8,192,128]{2,1,0:T(8,128)(2,1)S(1)}, bf16[8,192,128]{2,1,0:T(8,128)(2,1)S(1)}, bf16[8,192,128]{2,1,0:T(8,128)(2,1)S(1)}, bf16[8,192,128]{2,1,0:T(8,128)(2,1)S(1)}) custom-call(s32[4]{0:T(128)S(1)} %get-tuple-element.126.info_ref, bf16[8,384,128]{2,1,0:T(8,128)(2,1)S(1)} %get-tuple-element.127.refs_0_, ...), custom_call_target="tpu_custom_call" | custom-call | flops 19327352832 | bytes 3145728 | tf_op jit(solution)/shard_map/pallas_call | solution.py:133
  407.3 3.6 collective-permute-done.22
  410.9 6.6 %collective-permute-done.23 = bf16[8,192,128]{2,1,0:T(8,128)(2,1)S(1)} collective-permute-done((bf16[8,192,128]{2,1,0:T(8,128)(2,1)S(1)}, bf16[8,192,128]{2,1,0:T(8,128)(2,1)S(1)}, u32[]{:S(2)}, u32[]{:S(2)}) %collective-permute-start.23) | collective-permute-done | bytes 393248 | tf_op jit(solution)/shard_map/ppermute | solution.py:228
  417.6 3.7 copy-done.4
  (140 shorter events, 29.8 us)
Async XLA Ops:
  6.5 125.5 %all-gather.4.cloned.1.call-start = ((), (), s32[]{:S(2)}) async-start(), calls=%async_computation | async-start | bytes 5308416 | tf_op jit(solution)/shard_map/all_gather | solution.py:207
  13.0 32.4 %collective-permute-start = (bf16[8,384,128]{2,1,0:T(8,128)(2,1)}, bf16[8,384,128]{2,1,0:T(8,128)(2,1)}, u32[]{:S(2)}, u32[]{:S(2)}) collective-permute-start(bf16[8,384,128]{2,1,0:T(8,128)(2,1)} %get-tuple-element.71), channel_id=1, source_target_pairs={{0,2},{2,0},{1,3},{3,1},{4,6},{6,4},{5,7},{7,5},{8,10},{10,8},{9,1... | collective-permute-start | bytes 2359304 | tf_op jit(solution)/shard_map/ppermute | solution.py:203
  45.4 20.9 %collective-permute-start.5 = (bf16[8,384,128]{2,1,0:T(8,128)(2,1)}, bf16[8,384,128]{2,1,0:T(8,128)(2,1)}, u32[]{:S(2)}, u32[]{:S(2)}) collective-permute-start(bf16[8,384,128]{2,1,0:T(8,128)(2,1)} %get-tuple-element.140), channel_id=1, source_target_pairs={{0,2},{2,0},{1,3},{3,1},{4,6},{6,4},{5,7},{7,5},{8,10},{10,8},{9,1... | collective-permute-start | bytes 2359304 | tf_op jit(solution)/shard_map/ppermute | solution.py:203
  45.7 37.4 %collective-permute-start.6 = (bf16[8,384,128]{2,1,0:T(8,128)(2,1)}, bf16[8,384,128]{2,1,0:T(8,128)(2,1)}, u32[]{:S(2)}, u32[]{:S(2)}) collective-permute-start(bf16[8,384,128]{2,1,0:T(8,128)(2,1)} %get-tuple-element.138), channel_id=1, source_target_pairs={{0,2},{2,0},{1,3},{3,1},{4,6},{6,4},{5,7},{7,5},{8,10},{10,8},{9,1... | collective-permute-start | bytes 2359304 | tf_op jit(solution)/shard_map/ppermute | solution.py:203
  47.5 52.5 %collective-permute-start.7 = (bf16[8,384,128]{2,1,0:T(8,128)(2,1)}, bf16[8,384,128]{2,1,0:T(8,128)(2,1)}, u32[]{:S(2)}, u32[]{:S(2)}) collective-permute-start(bf16[8,384,128]{2,1,0:T(8,128)(2,1)} %get-tuple-element.136), channel_id=1, source_target_pairs={{0,2},{2,0},{1,3},{3,1},{4,6},{6,4},{5,7},{7,5},{8,10},{10,8},{9,1... | collective-permute-start | bytes 2359304 | tf_op jit(solution)/shard_map/ppermute | solution.py:203
  47.7 69.1 %collective-permute-start.8 = (bf16[8,384,128]{2,1,0:T(8,128)(2,1)}, bf16[8,384,128]{2,1,0:T(8,128)(2,1)}, u32[]{:S(2)}, u32[]{:S(2)}) collective-permute-start(bf16[8,384,128]{2,1,0:T(8,128)(2,1)} %get-tuple-element.135), channel_id=1, source_target_pairs={{0,2},{2,0},{1,3},{3,1},{4,6},{6,4},{5,7},{7,5},{8,10},{10,8},{9,1... | collective-permute-start | bytes 2359304 | tf_op jit(solution)/shard_map/ppermute | solution.py:203
  49.5 82.5 %collective-permute-start.1 = (bf16[8,384,128]{2,1,0:T(8,128)(2,1)}, bf16[8,384,128]{2,1,0:T(8,128)(2,1)}, u32[]{:S(2)}, u32[]{:S(2)}) collective-permute-start(bf16[8,384,128]{2,1,0:T(8,128)(2,1)} %get-tuple-element.76), channel_id=1, source_target_pairs={{0,2},{2,0},{1,3},{3,1},{4,6},{6,4},{5,7},{7,5},{8,10},{10,8},{9,1... | collective-permute-start | bytes 2359304 | tf_op jit(solution)/shard_map/ppermute | solution.py:203
  175.7 41.5 %collective-permute-start.10 = (bf16[8,192,128]{2,1,0:T(8,128)(2,1)S(1)}, bf16[8,192,128]{2,1,0:T(8,128)(2,1)S(1)}, u32[]{:S(2)}, u32[]{:S(2)}) collective-permute-start(bf16[8,192,128]{2,1,0:T(8,128)(2,1)S(1)} %get-tuple-element.91), channel_id=1, source_target_pairs={{0,2},{1,3},{2,0},{3,1},{4,6},{5,7},{6,4},{7,5},{8,10},{9,11},{10,... | collective-permute-start | bytes 1179656 | tf_op jit(solution)/shard_map/ppermute | solution.py:228
  176.3 42.3 %collective-permute-start.11 = (bf16[8,192,128]{2,1,0:T(8,128)(2,1)S(1)}, bf16[8,192,128]{2,1,0:T(8,128)(2,1)S(1)}, u32[]{:S(2)}, u32[]{:S(2)}) collective-permute-start(bf16[8,192,128]{2,1,0:T(8,128)(2,1)S(1)} %get-tuple-element.92), channel_id=1, source_target_pairs={{0,3},{1,2},{2,1},{3,0},{4,7},{5,6},{6,5},{7,4},{8,11},{9,10},{10,... | collective-permute-start | bytes 1179656 | tf_op jit(solution)/shard_map/ppermute | solution.py:228
  176.3 42.3 %collective-permute-start.9 = (bf16[8,192,128]{2,1,0:T(8,128)(2,1)S(1)}, bf16[8,192,128]{2,1,0:T(8,128)(2,1)S(1)}, u32[]{:S(2)}, u32[]{:S(2)}) collective-permute-start(bf16[8,192,128]{2,1,0:T(8,128)(2,1)S(1)} %get-tuple-element.90), channel_id=1, source_target_pairs={{0,1},{1,0},{2,3},{3,2},{4,5},{5,4},{6,7},{7,6},{8,9},{9,8},{10,11... | collective-permute-start | bytes 1179656 | tf_op jit(solution)/shard_map/ppermute | solution.py:228
  216.6 41.8 %collective-permute-start.2 = (bf16[8,192,128]{2,1,0:T(8,128)(2,1)S(1)}, bf16[8,192,128]{2,1,0:T(8,128)(2,1)S(1)}, u32[]{:S(2)}, u32[]{:S(2)}) collective-permute-start(bf16[8,192,128]{2,1,0:T(8,128)(2,1)S(1)} %get-tuple-element.79), channel_id=1, source_target_pairs={{0,1},{1,0},{2,3},{3,2},{4,5},{5,4},{6,7},{7,6},{8,9},{9,8},{10,11... | collective-permute-start | bytes 1179656 | tf_op jit(solution)/shard_map/ppermute | solution.py:228
  216.7 42.7 %collective-permute-start.3 = (bf16[8,192,128]{2,1,0:T(8,128)(2,1)S(1)}, bf16[8,192,128]{2,1,0:T(8,128)(2,1)S(1)}, u32[]{:S(2)}, u32[]{:S(2)}) collective-permute-start(bf16[8,192,128]{2,1,0:T(8,128)(2,1)S(1)} %get-tuple-element.80), channel_id=1, source_target_pairs={{0,2},{1,3},{2,0},{3,1},{4,6},{5,7},{6,4},{7,5},{8,10},{9,11},{10,... | collective-permute-start | bytes 1179656 | tf_op jit(solution)/shard_map/ppermute | solution.py:228
  217.3 42.2 %collective-permute-start.4 = (bf16[8,192,128]{2,1,0:T(8,128)(2,1)S(1)}, bf16[8,192,128]{2,1,0:T(8,128)(2,1)S(1)}, u32[]{:S(2)}, u32[]{:S(2)}) collective-permute-start(bf16[8,192,128]{2,1,0:T(8,128)(2,1)S(1)} %get-tuple-element.81), channel_id=1, source_target_pairs={{0,3},{1,2},{2,1},{3,0},{4,7},{5,6},{6,5},{7,4},{8,11},{9,10},{10,... | collective-permute-start | bytes 1179656 | tf_op jit(solution)/shard_map/ppermute | solution.py:228
  257.5 44.8 %collective-permute-start.15 = (bf16[8,192,128]{2,1,0:T(8,128)(2,1)S(1)}, bf16[8,192,128]{2,1,0:T(8,128)(2,1)}, u32[]{:S(2)}, u32[]{:S(2)}) collective-permute-start(bf16[8,192,128]{2,1,0:T(8,128)(2,1)S(1)} %get-tuple-element.112), channel_id=1, source_target_pairs={{0,1},{1,0},{2,3},{3,2},{4,5},{5,4},{6,7},{7,6},{8,9},{9,8},{10,11... | collective-permute-start | bytes 1179656 | tf_op jit(solution)/shard_map/ppermute | solution.py:228
  257.9 45.4 %collective-permute-start.16 = (bf16[8,192,128]{2,1,0:T(8,128)(2,1)S(1)}, bf16[8,192,128]{2,1,0:T(8,128)(2,1)}, u32[]{:S(2)}, u32[]{:S(2)}) collective-permute-start(bf16[8,192,128]{2,1,0:T(8,128)(2,1)S(1)} %get-tuple-element.113), channel_id=1, source_target_pairs={{0,2},{1,3},{2,0},{3,1},{4,6},{5,7},{6,4},{7,5},{8,10},{9,11},{10,... | collective-permute-start | bytes 1179656 | tf_op jit(solution)/shard_map/ppermute | solution.py:228
  258.4 44.9 %collective-permute-start.17 = (bf16[8,192,128]{2,1,0:T(8,128)(2,1)S(1)}, bf16[8,192,128]{2,1,0:T(8,128)(2,1)S(1)}, u32[]{:S(2)}, u32[]{:S(2)}) collective-permute-start(bf16[8,192,128]{2,1,0:T(8,128)(2,1)S(1)} %get-tuple-element.114), channel_id=1, source_target_pairs={{0,3},{1,2},{2,1},{3,0},{4,7},{5,6},{6,5},{7,4},{8,11},{9,10},{10,... | collective-permute-start | bytes 1179656 | tf_op jit(solution)/shard_map/ppermute | solution.py:228
  298.9 12.0 %collective-permute-start.13 = (bf16[8,192,128]{2,1,0:T(8,128)(2,1)S(1)}, bf16[8,192,128]{2,1,0:T(8,128)(2,1)S(1)}, u32[]{:S(2)}, u32[]{:S(2)}) collective-permute-start(bf16[8,192,128]{2,1,0:T(8,128)(2,1)S(1)} %get-tuple-element.102), channel_id=1, source_target_pairs={{0,2},{1,3},{2,0},{3,1},{4,6},{5,7},{6,4},{7,5},{8,10},{9,11},{10,... | collective-permute-start | bytes 1179656 | tf_op jit(solution)/shard_map/ppermute | solution.py:228
  302.2 15.3 %collective-permute-start.14 = (bf16[8,192,128]{2,1,0:T(8,128)(2,1)S(1)}, bf16[8,192,128]{2,1,0:T(8,128)(2,1)S(1)}, u32[]{:S(2)}, u32[]{:S(2)}) collective-permute-start(bf16[8,192,128]{2,1,0:T(8,128)(2,1)S(1)} %get-tuple-element.103), channel_id=1, source_target_pairs={{0,3},{1,2},{2,1},{3,0},{4,7},{5,6},{6,5},{7,4},{8,11},{9,10},{10,... | collective-permute-start | bytes 1179656 | tf_op jit(solution)/shard_map/ppermute | solution.py:228
  357.2 45.8 %collective-permute-start.18 = (bf16[8,192,128]{2,1,0:T(8,128)(2,1)S(1)}, bf16[8,192,128]{2,1,0:T(8,128)(2,1)}, u32[]{:S(2)}, u32[]{:S(2)}) collective-permute-start(bf16[8,192,128]{2,1,0:T(8,128)(2,1)S(1)} %get-tuple-element.123), channel_id=1, source_target_pairs={{0,1},{1,0},{2,3},{3,2},{4,5},{5,4},{6,7},{7,6},{8,9},{9,8},{10,11... | collective-permute-start | bytes 1179656 | tf_op jit(solution)/shard_map/ppermute | solution.py:228
  358.0 47.0 %collective-permute-start.19 = (bf16[8,192,128]{2,1,0:T(8,128)(2,1)S(1)}, bf16[8,192,128]{2,1,0:T(8,128)(2,1)}, u32[]{:S(2)}, u32[]{:S(2)}) collective-permute-start(bf16[8,192,128]{2,1,0:T(8,128)(2,1)S(1)} %get-tuple-element.124), channel_id=1, source_target_pairs={{0,2},{1,3},{2,0},{3,1},{4,6},{5,7},{6,4},{7,5},{8,10},{9,11},{10,... | collective-permute-start | bytes 1179656 | tf_op jit(solution)/shard_map/ppermute | solution.py:228
  358.5 47.5 %collective-permute-start.20 = (bf16[8,192,128]{2,1,0:T(8,128)(2,1)S(1)}, bf16[8,192,128]{2,1,0:T(8,128)(2,1)}, u32[]{:S(2)}, u32[]{:S(2)}) collective-permute-start(bf16[8,192,128]{2,1,0:T(8,128)(2,1)S(1)} %get-tuple-element.125), channel_id=1, source_target_pairs={{0,3},{1,2},{2,1},{3,0},{4,7},{5,6},{6,5},{7,4},{8,11},{9,10},{10,... | collective-permute-start | bytes 1179656 | tf_op jit(solution)/shard_map/ppermute | solution.py:228
  398.1 9.1 %collective-permute-start.21 = (bf16[8,192,128]{2,1,0:T(8,128)(2,1)S(1)}, bf16[8,192,128]{2,1,0:T(8,128)(2,1)S(1)}, u32[]{:S(2)}, u32[]{:S(2)}) collective-permute-start(bf16[8,192,128]{2,1,0:T(8,128)(2,1)S(1)} %get-tuple-element.130), channel_id=1, source_target_pairs={{0,1},{1,0},{2,3},{3,2},{4,5},{5,4},{6,7},{7,6},{8,9},{9,8},{10,11... | collective-permute-start | bytes 1179656 | tf_op jit(solution)/shard_map/ppermute | solution.py:228
  398.9 12.0 %collective-permute-start.22 = (bf16[8,192,128]{2,1,0:T(8,128)(2,1)S(1)}, bf16[8,192,128]{2,1,0:T(8,128)(2,1)S(1)}, u32[]{:S(2)}, u32[]{:S(2)}) collective-permute-start(bf16[8,192,128]{2,1,0:T(8,128)(2,1)S(1)} %get-tuple-element.131), channel_id=1, source_target_pairs={{0,2},{1,3},{2,0},{3,1},{4,6},{5,7},{6,4},{7,5},{8,10},{9,11},{10,... | collective-permute-start | bytes 1179656 | tf_op jit(solution)/shard_map/ppermute | solution.py:228
  403.0 14.5 %collective-permute-start.23 = (bf16[8,192,128]{2,1,0:T(8,128)(2,1)S(1)}, bf16[8,192,128]{2,1,0:T(8,128)(2,1)S(1)}, u32[]{:S(2)}, u32[]{:S(2)}) collective-permute-start(bf16[8,192,128]{2,1,0:T(8,128)(2,1)S(1)} %get-tuple-element.132), channel_id=1, source_target_pairs={{0,3},{1,2},{2,1},{3,0},{4,7},{5,6},{6,5},{7,4},{8,11},{9,10},{10,... | collective-permute-start | bytes 1179656 | tf_op jit(solution)/shard_map/ppermute | solution.py:228
  (30 other events, 829.9 us)
Sparse Core Ops, SparseCore 0:
  45.5 51.9 all-gather.3
